TPU v7x, 32 devices: a whole 2x2x4 slice. The times are simulated.
32 devices in a mesh: dp: 8 (over z, core), expert: 4 (over y, x).
Axes of the slice: x: 2, y: 2, z: 4, core: 2. Of those that a mesh axis runs over, the one named last changes fastest.
Arguments:
- tokens: bfloat16 [4096, 2048], P(('dp', 'expert')), may hold values from -6 to 6
- norm_gain: float32 [2048], replicated, may hold values from 0.25 to 1.75
- router_weight: bfloat16 [2048, 64], P('dp'), may hold values from -0.25 to 0.25
- expert_ids: int32 [4096, 8], P(('dp', 'expert')), may hold values from 0 to 63, all different within a row; in each aligned block of 128 rows (0 to 127, 128 to 255, ...) at most 32 rows name the same one
- gate_weight: bfloat16 [4, 2048, 1024], P('expert', 'dp'), may hold values from -0.125 to 0.125
- up_weight: bfloat16 [4, 2048, 1024], P('expert', 'dp'), may hold values from -0.125 to 0.125
- down_weight: bfloat16 [4, 2048, 1024], P('expert', 'dp'), may hold values from -0.1875 to 0.1875
- cotangent: bfloat16 [4096, 2048], P(('dp', 'expert')), may hold values from -6 to 6
Outputs:
- mixed: bfloat16 [4096, 2048], P(('dp', 'expert'))
- d_tokens: bfloat16 [4096, 2048], P(('dp', 'expert'))
- d_gain: float32 [2048], replicated
- d_router: float32 [2048, 64], P('dp')
- d_gate: bfloat16 [4, 2048, 1024], P('expert', 'dp')
- d_up: bfloat16 [4, 2048, 1024], P('expert', 'dp')
- d_down: bfloat16 [4, 2048, 1024], P('expert', 'dp')
Inputs may be any that keep to these rules, and one draw needn't show every extreme that they name: `expert_ids`: each row names 8 different experts; in the rows of one device no expert is named more than 32 times.
All inputs are finite; a program needn't handle non-finite values.
Results may differ from a plain program's by a relative error of at most 0.018.
Values may be sent and summed in bfloat16 or wider, within the bound.
A program may use at most 128 MiB of HBM per device.

v0:
```python
import jax
import jax.numpy as jnp
from jax import lax
from jax.sharding import PartitionSpec as P

D = 2048
FF = 1024
CAP = 32


EPSILON = 1e-05
HIGHEST = lax.Precision.HIGHEST


def normalize(inputs, norm_gain):
    meansq = jnp.mean(inputs * inputs, axis=-1, keepdims=True)
    return inputs * lax.rsqrt(meansq + EPSILON) * norm_gain


def gate_weights(logits, expert_ids):
    member = (
        expert_ids[:, :, None] == jnp.arange(logits.shape[-1], dtype=jnp.int32)[None, None, :]
    ).astype(jnp.float32)
    picked = jnp.sum(member * logits[:, None, :], axis=-1)
    raised = jnp.exp(picked)
    return raised / jnp.sum(raised, axis=-1, keepdims=True)


def pick_matrix(expert_ids, window, capacity):
    flat_ids = expert_ids.reshape(-1)
    chosen = (flat_ids[:, None] == jnp.arange(window, dtype=jnp.int32)[None, :]).astype(jnp.int32)
    before = jnp.cumsum(chosen, axis=0, dtype=jnp.int32) - chosen
    position = jnp.sum(before * chosen, axis=-1)
    target = jnp.where(flat_ids < window, flat_ids * capacity + position, -1)
    columns = jnp.arange(window * capacity, dtype=jnp.int32)
    matrix = (target[:, None] == columns[None, :]).astype(jnp.float32)
    return matrix.reshape(expert_ids.shape[0], expert_ids.shape[1], window * capacity)


def expert_forward(slot_rows, w_gate, w_up, w_down):
    gate_pre = jnp.dot(slot_rows, w_gate, preferred_element_type=jnp.float32)
    up_pre = jnp.dot(slot_rows, w_up, preferred_element_type=jnp.float32)
    active = (gate_pre * jax.nn.sigmoid(gate_pre) * up_pre).astype(jnp.bfloat16)
    output = jnp.dot(active, w_down.T, preferred_element_type=jnp.float32).astype(jnp.bfloat16)
    return (output, gate_pre, up_pre)


def expert_backward(slot_grads, gate_pre, up_pre, w_gate, w_up, w_down):
    sigmoid_gate = jax.nn.sigmoid(gate_pre)
    active = (gate_pre * sigmoid_gate * up_pre).astype(jnp.bfloat16)
    back = jnp.dot(slot_grads, w_down, preferred_element_type=jnp.float32)
    grad_gate = (back * up_pre * sigmoid_gate * (1.0 + gate_pre * (1.0 - sigmoid_gate))).astype(
        jnp.bfloat16
    )
    grad_upper = (back * gate_pre * sigmoid_gate).astype(jnp.bfloat16)
    grad_rows = jnp.dot(grad_gate, w_gate.T, preferred_element_type=jnp.float32)
    grad_rows = (
        grad_rows + jnp.dot(grad_upper, w_up.T, preferred_element_type=jnp.float32)
    ).astype(jnp.bfloat16)
    return (grad_rows, active, grad_gate, grad_upper)


def group_terms(slot_rows, slot_grads, active, grad_gate, grad_upper):
    term_gate = jnp.einsum("krd,krf->kdf", slot_rows, grad_gate, preferred_element_type=jnp.float32)
    term_upper = jnp.einsum(
        "krd,krf->kdf", slot_rows, grad_upper, preferred_element_type=jnp.float32
    )
    term_down = jnp.einsum("krd,krf->kdf", slot_grads, active, preferred_element_type=jnp.float32)
    stacked = jnp.concatenate([term_gate, term_upper, term_down], axis=-1)
    rounded = lax.optimization_barrier(stacked.astype(jnp.bfloat16)).astype(jnp.float32)
    return jnp.sum(rounded, axis=0)


def body(
    tokens, norm_gain, router_weight, expert_ids, gate_weight, up_weight, down_weight, cotangent
):
    window = lax.axis_size("expert")
    groups_dp = lax.axis_size("dp")
    slot_count = window * CAP
    router_full = lax.all_gather(router_weight, "dp", axis=0, tiled=True)
    inputs = tokens.astype(jnp.float32)
    hidden = normalize(inputs, norm_gain).astype(jnp.bfloat16)
    logits = jnp.dot(hidden, router_full, preferred_element_type=jnp.float32)
    weights, gate_back = jax.vjp(lambda values: gate_weights(values, expert_ids), logits)
    pick_table = pick_matrix(expert_ids, window, CAP)
    spread_half = jnp.sum(pick_table, axis=1).astype(jnp.bfloat16)
    blending = jnp.einsum("tks,tk->ts", pick_table, weights, precision=HIGHEST)
    outgoing = (
        jnp.dot(spread_half.T, hidden, preferred_element_type=jnp.float32)
        .astype(jnp.bfloat16)
        .reshape(window, CAP, D)
    )
    weights_full = (
        lax.all_gather(gate_weight, "dp", axis=1, tiled=True),
        lax.all_gather(up_weight, "dp", axis=1, tiled=True),
        lax.all_gather(down_weight, "dp", axis=1, tiled=True),
    )
    w_gate = weights_full[0][0]
    w_up = weights_full[1][0]
    w_down = weights_full[2][0]
    arrived_rows = lax.all_to_all(outgoing, "expert", split_axis=0, concat_axis=0, tiled=True)
    lead = arrived_rows.shape[0]
    middle = arrived_rows.shape[1]
    output, gate_pre, up_pre = expert_forward(arrived_rows.reshape(-1, D), w_gate, w_up, w_down)
    produced = output.reshape(lead, middle, D)
    gate_slots = gate_pre.reshape(lead, middle, FF)
    upper_slots = up_pre.reshape(lead, middle, FF)
    returned = lax.all_to_all(produced, "expert", split_axis=0, concat_axis=0, tiled=True).reshape(
        slot_count, D
    )
    returned_wide = returned.astype(jnp.float32)
    mixed_out = jnp.dot(blending, returned_wide, precision=HIGHEST).astype(jnp.bfloat16)
    gathered_cot = jnp.dot(spread_half.T, cotangent, preferred_element_type=jnp.float32)
    per_slot = jnp.sum(gathered_cot * returned_wide, axis=-1)
    grad_weights = jnp.einsum("tks,s->tk", pick_table, per_slot, precision=HIGHEST)
    grad_logits = gate_back(grad_weights)[0]
    outgoing_grad = (
        jnp.dot(blending.T, cotangent.astype(jnp.float32), precision=HIGHEST)
        .astype(jnp.bfloat16)
        .reshape(window, CAP, D)
    )
    arrived_grad = lax.all_to_all(outgoing_grad, "expert", split_axis=0, concat_axis=0, tiled=True)
    flat_rows = arrived_rows.reshape(-1, D)
    flat_grads = arrived_grad.reshape(-1, D)
    grad_rows, active, grad_gate, grad_upper = expert_backward(
        flat_grads, gate_slots.reshape(-1, FF), upper_slots.reshape(-1, FF), w_gate, w_up, w_down
    )
    grad_back = lax.all_to_all(
        grad_rows.reshape(window, CAP, D), "expert", split_axis=0, concat_axis=0, tiled=True
    ).reshape(slot_count, D)
    shard_rows = D // groups_dp
    rows_cut, grads_cut = (
        lax.all_to_all(flat_rows, "dp", split_axis=1, concat_axis=0, tiled=True),
        lax.all_to_all(flat_grads, "dp", split_axis=1, concat_axis=0, tiled=True),
    )
    per_group = flat_rows.shape[0]
    pieces = (
        lax.all_gather(grad_gate, "dp", axis=0, tiled=True),
        lax.all_gather(grad_upper, "dp", axis=0, tiled=True),
        lax.all_gather(active, "dp", axis=0, tiled=True),
    )
    extent = pieces[0].shape[0]
    groups_in = extent // per_group
    rows_part = rows_cut.reshape(groups_in, per_group, shard_rows)
    grads_part = grads_cut.reshape(groups_in, per_group, shard_rows)
    gate_part = pieces[0].reshape(groups_in, per_group, FF)
    upper_part = pieces[1].reshape(groups_in, per_group, FF)
    active_part = pieces[2].reshape(groups_in, per_group, FF)
    summed = group_terms(rows_part, grads_part, active_part, gate_part, upper_part)
    grad_hidden = jnp.dot(spread_half, grad_back, preferred_element_type=jnp.float32)
    grad_hidden = grad_hidden + jnp.dot(
        grad_logits, router_full.astype(jnp.float32).T, precision=HIGHEST
    )
    unused_value, norm_back = jax.vjp(normalize, inputs, norm_gain)
    grad_inputs, grad_gain = norm_back(grad_hidden)
    grad_router = jnp.dot(hidden.astype(jnp.float32).T, grad_logits, precision=HIGHEST)
    router_part = lax.psum_scatter(
        grad_router.astype(jnp.bfloat16), "dp", scatter_dimension=0, tiled=True
    )
    router_mine = lax.psum(router_part, "expert").astype(jnp.float32)
    gain_sum = lax.psum(grad_gain, ("dp", "expert"))
    grad_gate_out = summed[:, :FF].astype(jnp.bfloat16)[None]
    grad_up_out = summed[:, FF : 2 * FF].astype(jnp.bfloat16)[None]
    grad_down_out = summed[:, 2 * FF :].astype(jnp.bfloat16)[None]
    return (
        mixed_out,
        grad_inputs.astype(jnp.bfloat16),
        gain_sum,
        router_mine,
        grad_gate_out,
        grad_up_out,
        grad_down_out,
    )


def solution(mesh):
    in_specs = (
        P(("dp", "expert"), None),
        P(),
        P("dp", None),
        P(("dp", "expert"), None),
        P("expert", "dp", None),
        P("expert", "dp", None),
        P("expert", "dp", None),
        P(("dp", "expert"), None),
    )
    out_specs = (
        P(("dp", "expert"), None),
        P(("dp", "expert"), None),
        P(),
        P("dp", None),
        P("expert", "dp", None),
        P("expert", "dp", None),
        P("expert", "dp", None),
    )
    return jax.shard_map(body, mesh=mesh, in_specs=in_specs, out_specs=out_specs, check_vma=False)
```

profile of v0, /device:TPU:0, one launch (start us, length us, event | category | flops | bytes accessed | tf_op | source)
XLA Modules:
  0.0 339.7 jit_solution(7952552429627518324)
XLA Ops:
  13.0 16.8 %all_gather.21 = bf16[2048,64]{0,1:T(8,128)(2,1)S(1)} all-gather(bf16[256,64]{0,1:T(8,128)(2,1)} %param.10), channel_id=1, replica_groups=mesh['dp'=8,'expert'=4] {'dp'}, dimensions={0}, use_global_device_ids=true | all-gather | bytes 294912 | tf_op jit(solution)/shard_map/all_gather | solution.py:80
  35.5 3.7 %all-to-all-start.2 = ((bf16[4,32,2048]{2,1,0:T(8,128)(2,1)}), bf16[4,32,2048]{2,1,0:T(8,128)(2,1)S(1)}, u32[]{:S(2)}, u32[]{:S(2)}) async-start(bf16[4,32,2048]{2,1,0:T(8,128)(2,1)} %bitcast.11), calls=%async_computation.2 | async-start | bytes 1048576 | tf_op jit(solution)/shard_map/all_to_all | solution.py:122
  40.7 7.1 %all-to-all-done.2 = bf16[4,32,2048]{2,1,0:T(8,128)(2,1)S(1)} async-done(((bf16[4,32,2048]{2,1,0:T(8,128)(2,1)}), bf16[4,32,2048]{2,1,0:T(8,128)(2,1)S(1)}, u32[]{:S(2)}, u32[]{:S(2)}) %all-to-all-start.2) | async-done | bytes 524320 | tf_op jit(solution)/shard_map/all_to_all | solution.py:122
  47.8 3.5 %all-to-all-start = ((bf16[4,32,2048]{2,1,0:T(8,128)(2,1)}), bf16[4,32,2048]{2,1,0:T(8,128)(2,1)S(1)}, u32[]{:S(2)}, u32[]{:S(2)}) async-start(bf16[4,32,2048]{2,1,0:T(8,128)(2,1)} %bitcast.4), calls=%async_computation | async-start | bytes 1048576 | tf_op jit(solution)/shard_map/all_to_all | solution.py:101
  51.2 9.3 %all-gather.11.cloned.1.call-done = bf16[1,2048,1024]{2,1,0:T(8,128)(2,1)} async-done(((bf16[1,256,1024]{2,1,0:T(8,128)(2,1)}), bf16[1,2048,1024]{2,1,0:T(8,128)(2,1)}) %all-gather.11.cloned.1.call-update) | async-done | bytes 4194320 | tf_op jit(solution)/shard_map/all_gather | solution.py:96
  63.5 44.9 %all-gather.9.cloned.1.call-done = bf16[1,2048,1024]{2,1,0:T(8,128)(2,1)} async-done(((bf16[1,256,1024]{2,1,0:T(8,128)(2,1)}), bf16[1,2048,1024]{2,1,0:T(8,128)(2,1)}) %all-gather.9.cloned.1.call-update) | async-done | bytes 4194320 | tf_op jit(solution)/shard_map/all_gather | solution.py:95
  111.3 44.6 %all-gather.7.cloned.1.call-done = bf16[1,2048,1024]{2,1,0:T(8,128)(2,1)} async-done(((bf16[1,256,1024]{2,1,0:T(8,128)(2,1)}), bf16[1,2048,1024]{2,1,0:T(8,128)(2,1)}) %all-gather.7.cloned.1.call-update) | async-done | bytes 4194320 | tf_op jit(solution)/shard_map/all_gather | solution.py:94
  155.9 4.0 %multiply_convert_fusion.1 = (bf16[128,1024]{1,0:T(8,128)(2,1)}, bf16[128,1024]{1,0:T(8,128)(2,1)S(1)}, bf16[128,1024]{1,0:T(8,128)(2,1)}) fusion(f32[128,1024]{1,0:T(8,128)S(1)} %fusion, f32[128,1024]{1,0:T(8,128)S(1)} %fusion.6, bf16[128,2048]{1,0:T(8,128)(2,1)S(1)} %bitcast.117, bf16[1,2048,1024]{2,1,0:T(8,128)(2,1)} %all-gather.7.cloned.1.call-done), kind=kOutput, calls=%fused_computation.45 | convolution fusion | flops 538968064 | bytes 6553600 | tf_op jit(solution)/shard_map/dot_general | solution.py:41
  159.8 4.6 %fusion.18 = bf16[128,2048]{1,0:T(8,128)(2,1)} fusion(bf16[128,1024]{1,0:T(8,128)(2,1)S(1)} %get-tuple-element.13, bf16[1,2048,1024]{2,1,0:T(8,128)(2,1)} %all-gather.11.cloned.1.call-done), kind=kOutput, calls=%fused_computation.20 | convolution fusion | flops 537133056 | bytes 4980736 | tf_op jit(solution)/shard_map/dot_general | solution.py:44
  164.4 3.6 %all-to-all-start.1 = ((bf16[4,32,2048]{2,1,0:T(8,128)(2,1)}), bf16[4,32,2048]{2,1,0:T(8,128)(2,1)S(1)}, u32[]{:S(2)}, u32[]{:S(2)}) async-start(bf16[4,32,2048]{2,1,0:T(8,128)(2,1)} %bitcast.9), calls=%async_computation.1 | async-start | bytes 1048576 | tf_op jit(solution)/shard_map/all_to_all | solution.py:108
  168.1 8.5 %all-to-all-done.1 = bf16[4,32,2048]{2,1,0:T(8,128)(2,1)S(1)} async-done(((bf16[4,32,2048]{2,1,0:T(8,128)(2,1)}), bf16[4,32,2048]{2,1,0:T(8,128)(2,1)S(1)}, u32[]{:S(2)}, u32[]{:S(2)}) %all-to-all-start.1) | async-done | bytes 524320 | tf_op jit(solution)/shard_map/all_to_all | solution.py:108
  177.0 5.1 %fusion.32 = f32[1,128,8]{2,0,1:T(1,128)} fusion(s32[128,8]{1,0:T(8,128)} %copy-done.9, f32[128]{0:T(128)S(1)} %fusion.23), kind=kOutput, calls=%fused_computation.50 | convolution fusion | flops 1703936 | bytes 8704 | tf_op jit(solution)/shard_map/tks,s->tk/dot_general | solution.py:115
  186.3 3.9 %fusion.4 = f32[128,2048]{1,0:T(8,128)S(1)} fusion(bf16[128,1024]{1,0:T(8,128)(2,1)S(1)} %copy-done.8, bf16[1,2048,1024]{2,1,0:T(8,128)(2,1)} %all-gather.9.cloned.1.call-done), kind=kOutput, calls=%fused_computation.5 | convolution fusion | flops 536870912 | bytes 5505024 | tf_op jit(solution)/shard_map/dot_general | solution.py:58
  192.5 3.6 %all-to-all-start.3 = ((bf16[4,32,2048]{2,1,0:T(8,128)(2,1)}), bf16[4,32,2048]{2,1,0:T(8,128)(2,1)S(1)}, u32[]{:S(2)}, u32[]{:S(2)}) async-start(bf16[4,32,2048]{2,1,0:T(8,128)(2,1)} %bitcast.122), calls=%async_computation.3 | async-start | bytes 1048576 | tf_op jit(solution)/shard_map/all_to_all | solution.py:128
  203.7 3.5 %all-to-all-start.4 = ((bf16[128,8,256]{0,2,1:T(8,128)(2,1)}), bf16[128,8,256]{0,2,1:T(8,128)(2,1)S(1)}, u32[]{:S(2)}, u32[]{:S(2)}) async-start(bf16[128,8,256]{0,2,1:T(8,128)(2,1)} %copy.42), calls=%async_computation.5 | async-start | bytes 1048576 | tf_op jit(solution)/shard_map/all_to_all | solution.py:133
  209.6 13.1 %all-to-all-done.4 = bf16[128,8,256]{0,2,1:T(8,128)(2,1)S(1)} async-done(((bf16[128,8,256]{0,2,1:T(8,128)(2,1)}), bf16[128,8,256]{0,2,1:T(8,128)(2,1)S(1)}, u32[]{:S(2)}, u32[]{:S(2)}) %all-to-all-start.4) | async-done | bytes 524320 | tf_op jit(solution)/shard_map/all_to_all | solution.py:133
  222.6 3.5 %all-to-all-start.5 = ((bf16[128,8,256]{0,2,1:T(8,128)(2,1)}), bf16[128,8,256]{0,2,1:T(8,128)(2,1)S(1)}, u32[]{:S(2)}, u32[]{:S(2)}) async-start(bf16[128,8,256]{0,2,1:T(8,128)(2,1)} %copy.43), calls=%async_computation.6 | async-start | bytes 1048576 | tf_op jit(solution)/shard_map/all_to_all | solution.py:134
  227.5 44.7 %psum.14 = f32[2048]{0:T(1024)} all-reduce(f32[2048]{0:T(1024)S(1)} %get-tuple-element.7), channel_id=1, replica_groups=mesh['dp'=8,'expert'=4] {'dp','expert'}, use_global_device_ids=true, to_apply=%region_12.13 | all-reduce | flops 2048 | bytes 16384 | tf_op jit(solution)/shard_map/psum | solution.py:161
  272.1 17.1 %psum.15 = bf16[256,64]{0,1:T(8,128)(2,1)S(1)} all-reduce(bf16[256,64]{0,1:T(8,128)(2,1)} %reduce-scatter.2.cloned.1.call-done), channel_id=1, replica_groups=mesh['dp'=8,'expert'=4] {'expert'}, use_global_device_ids=true, to_apply=%region_14.15 | all-reduce | flops 16384 | bytes 65536 | tf_op jit(solution)/shard_map/psum | solution.py:160
  289.9 4.8 %convolution_convert_fusion.1 = bf16[8,256,1024]{2,1,0:T(8,128)(2,1)} fusion(bf16[8,128,1024]{2,1,0:T(8,128)(2,1)} %bitcast.123, bf16[128,8,256]{0,2,1:T(8,128)(2,1)S(1)} %all-to-all-done.4), kind=kOutput, calls=%fused_computation.14 | convolution fusion | flops 538968064 | bytes 6815744 | tf_op jit(solution)/shard_map/krd,krf->kdf/dot_general | solution.py:65
  294.7 4.8 %convolution_convert_fusion.2 = bf16[8,256,1024]{2,1,0:T(8,128)(2,1)} fusion(bf16[8,128,1024]{2,1,0:T(8,128)(2,1)} %bitcast.125, bf16[128,8,256]{0,2,1:T(8,128)(2,1)S(1)} %all-to-all-done.4), kind=kOutput, calls=%fused_computation.15 | convolution fusion | flops 538968064 | bytes 6815744 | tf_op jit(solution)/shard_map/krd,krf->kdf/dot_general | solution.py:64
  299.5 14.1 %all-gather.17.cloned.1.call-done = bf16[1024,1024]{1,0:T(8,128)(2,1)} async-done(((bf16[128,1024]{1,0:T(8,128)(2,1)}), bf16[1024,1024]{1,0:T(8,128)(2,1)}) %all-gather.17.cloned.1.call-update) | async-done | bytes 2097168 | tf_op jit(solution)/shard_map/all_gather | solution.py:140
  316.6 7.9 %pad_maximum_fusion = bf16[8,256,3072]{2,1,0:T(8,128)(2,1)} fusion(bf16[8,256,1024]{2,1,0:T(8,128)(2,1)S(1)} %convolution_convert_fusion, bf16[8,256,1024]{2,1,0:T(8,128)(2,1)S(1)} %copy-done.1, bf16[8,256,1024]{2,1,0:T(8,128)(2,1)} %convolution_convert_fusion.2), kind=kLoop, calls=%fused_computation | loop fusion | flops 37748736 | bytes 25165824 | tf_op jit(solution)/shard_map/concatenate | solution.py:69
  324.5 7.3 %reduce = bf16[256,3072]{1,0:T(8,128)(2,1)S(1)} reduce(bf16[8,256,3072]{2,1,0:T(8,128)(2,1)} %pad_maximum_fusion, bf16[]{:T(256)} %constant.30), dimensions={0}, to_apply=%region_15.16.clone | reduce | flops 5505024 | bytes 14155778 | tf_op jit(solution)/shard_map/reduce_sum | solution.py:71
  (95 shorter events, 41.5 us)
Async XLA Ops:
  7.2 26.9 %copy-start = (bf16[128,2048]{1,0:T(8,128)(2,1)S(1)}, bf16[128,2048]{1,0:T(8,128)(2,1)}, u32[]{:S(2)}) copy-start(bf16[128,2048]{1,0:T(8,128)(2,1)} %param.15) | copy-start | bytes 1572868
  7.2 32.3 %copy-start.2 = (bf16[128,2048]{1,0:T(8,128)(2,1)S(1)}, bf16[128,2048]{1,0:T(8,128)(2,1)}, u32[]{:S(2)}) copy-start(bf16[128,2048]{1,0:T(8,128)(2,1)} %param.8) | copy-start | bytes 1572868
  7.2 32.3 %copy-start.10 = (f32[2048]{0:T(1024)S(1)}, f32[2048]{0:T(1024)}, u32[]{:S(2)}) copy-start(f32[2048]{0:T(1024)} %param.9) | copy-start | bytes 24580
  7.2 53.3 %all-gather.11.cloned.1.call-start = ((), (), s32[]{:S(2)}) async-start(), calls=%async_computation.9 | async-start | bytes 4718592 | tf_op jit(solution)/shard_map/all_gather | solution.py:96
  7.9 100.4 %all-gather.9.cloned.1.call-start = ((), (), s32[]{:S(2)}) async-start(), calls=%async_computation.8 | async-start | bytes 4718592 | tf_op jit(solution)/shard_map/all_gather | solution.py:95
  8.7 147.2 %all-gather.7.cloned.1.call-start = ((), (), s32[]{:S(2)}) async-start(), calls=%async_computation.7 | async-start | bytes 4718592 | tf_op jit(solution)/shard_map/all_gather | solution.py:94
  13.0 34.7 %copy-start.9 = (s32[128,8]{1,0:T(8,128)}, s32[128,8]{1,0:T(8,128)S(1)}, u32[]{:S(2)}) copy-start(s32[128,8]{1,0:T(8,128)S(1)} %copy.41) | copy-start | bytes 12292
  31.1 32.3 %copy-start.12 = (f32[128]{0:T(128)}, f32[128]{0:T(128)S(1)}, u32[]{:S(2)}) copy-start(f32[128]{0:T(128)S(1)} %fusion.27) | copy-start | bytes 1540
  35.5 12.2 %all-to-all-start.2 = ((bf16[4,32,2048]{2,1,0:T(8,128)(2,1)}), bf16[4,32,2048]{2,1,0:T(8,128)(2,1)S(1)}, u32[]{:S(2)}, u32[]{:S(2)}) async-start(bf16[4,32,2048]{2,1,0:T(8,128)(2,1)} %bitcast.11), calls=%async_computation.2 | async-start | bytes 1048576 | tf_op jit(solution)/shard_map/all_to_all | solution.py:122
  47.8 15.7 %all-to-all-start = ((bf16[4,32,2048]{2,1,0:T(8,128)(2,1)}), bf16[4,32,2048]{2,1,0:T(8,128)(2,1)S(1)}, u32[]{:S(2)}, u32[]{:S(2)}) async-start(bf16[4,32,2048]{2,1,0:T(8,128)(2,1)} %bitcast.4), calls=%async_computation | async-start | bytes 1048576 | tf_op jit(solution)/shard_map/all_to_all | solution.py:101
  159.8 24.5 %copy-start.4 = (bf16[128,1024]{1,0:T(8,128)(2,1)}, bf16[128,1024]{1,0:T(8,128)(2,1)S(1)}, u32[]{:S(2)}) copy-start(bf16[128,1024]{1,0:T(8,128)(2,1)S(1)} %get-tuple-element.13) | copy-start | bytes 786436
  159.8 23.3 %copy-start.11 = (s32[128,8]{0,1:T(8,128)S(1)}, s32[128,8]{0,1:T(8,128)}, u32[]{:S(2)}) copy-start(s32[128,8]{0,1:T(8,128)} %param.11) | copy-start | bytes 12292
  159.8 26.5 %copy-start.8 = (bf16[128,1024]{1,0:T(8,128)(2,1)S(1)}, bf16[128,1024]{1,0:T(8,128)(2,1)}, u32[]{:S(2)}) copy-start(bf16[128,1024]{1,0:T(8,128)(2,1)} %get-tuple-element.14) | copy-start | bytes 786436
  164.4 12.1 %all-to-all-start.1 = ((bf16[4,32,2048]{2,1,0:T(8,128)(2,1)}), bf16[4,32,2048]{2,1,0:T(8,128)(2,1)S(1)}, u32[]{:S(2)}, u32[]{:S(2)}) async-start(bf16[4,32,2048]{2,1,0:T(8,128)(2,1)} %bitcast.9), calls=%async_computation.1 | async-start | bytes 1048576 | tf_op jit(solution)/shard_map/all_to_all | solution.py:108
  168.1 104.1 %reduce-scatter.2.cloned.1.call-start = ((), (), s32[]{:S(2)}) async-start(), calls=%async_computation.10 | async-start | bytes 294912 | tf_op jit(solution)/shard_map/reduce_scatter | solution.py:157
  177.0 13.2 %copy-start.5 = (bf16[128,1024]{1,0:T(8,128)(2,1)S(1)}, bf16[128,1024]{1,0:T(8,128)(2,1)}, u32[]{:S(2)}) copy-start(bf16[128,1024]{1,0:T(8,128)(2,1)} %get-tuple-element.12) | copy-start | bytes 786436
  184.4 105.5 %all-gather.15.cloned.1.call-start = ((), (), s32[]{:S(2)}) async-start(), calls=%async_computation.12 | async-start | bytes 2359296 | tf_op jit(solution)/shard_map/all_gather | solution.py:139
  185.0 109.7 %all-gather.13.cloned.1.call-start = ((), (), s32[]{:S(2)}) async-start(), calls=%async_computation.11 | async-start | bytes 2359296 | tf_op jit(solution)/shard_map/all_gather | solution.py:138
  185.5 128.1 %all-gather.17.cloned.1.call-start = ((), (), s32[]{:S(2)}) async-start(), calls=%async_computation.13 | async-start | bytes 2359296 | tf_op jit(solution)/shard_map/all_gather | solution.py:140
  192.5 15.0 %copy-start.7 = (bf16[2048,64]{0,1:T(8,128)(2,1)S(1)}, bf16[2048,64]{0,1:T(8,128)(2,1)}, u32[]{:S(2)}) copy-start(bf16[2048,64]{0,1:T(8,128)(2,1)} %copy-done.6) | copy-start | bytes 786436
  192.5 11.2 %all-to-all-start.3 = ((bf16[4,32,2048]{2,1,0:T(8,128)(2,1)}), bf16[4,32,2048]{2,1,0:T(8,128)(2,1)S(1)}, u32[]{:S(2)}, u32[]{:S(2)}) async-start(bf16[4,32,2048]{2,1,0:T(8,128)(2,1)} %bitcast.122), calls=%async_computation.3 | async-start | bytes 1048576 | tf_op jit(solution)/shard_map/all_to_all | solution.py:128
  197.0 11.4 %copy-start.13 = (f32[128]{0:T(128)S(1)}, f32[128]{0:T(128)}, u32[]{:S(2)}) copy-start(f32[128]{0:T(128)} %copy-done.12) | copy-start | bytes 1540
  203.7 18.9 %all-to-all-start.4 = ((bf16[128,8,256]{0,2,1:T(8,128)(2,1)}), bf16[128,8,256]{0,2,1:T(8,128)(2,1)S(1)}, u32[]{:S(2)}, u32[]{:S(2)}) async-start(bf16[128,8,256]{0,2,1:T(8,128)(2,1)} %copy.42), calls=%async_computation.5 | async-start | bytes 1048576 | tf_op jit(solution)/shard_map/all_to_all | solution.py:133
  222.6 76.9 %all-to-all-start.5 = ((bf16[128,8,256]{0,2,1:T(8,128)(2,1)}), bf16[128,8,256]{0,2,1:T(8,128)(2,1)S(1)}, u32[]{:S(2)}, u32[]{:S(2)}) async-start(bf16[128,8,256]{0,2,1:T(8,128)(2,1)} %copy.43), calls=%async_computation.6 | async-start | bytes 1048576 | tf_op jit(solution)/shard_map/all_to_all | solution.py:134
  (3 other events, 8.2 us)
Sparse Core Ops, SparseCore 0:
  9.6 50.8 all-gather.10
  62.1 46.1 all-gather.8
  110.0 45.8 all-gather.6
  184.5 28.2 reduce-scatter.1
  214.3 38.7 all-gather.14
  254.7 28.5 all-gather.12
  285.0 28.5 all-gather.16
where the time goes:
time: 341 us; the launch traced here: 340 us
  waiting for transfers between devices  148 us (43%)
  blocking collectives  78.5 us (23%)
  matrix products  47.1 us (14%)
  starting transfers between devices  21.8 us (6%)
  other arithmetic  21.4 us (6%)
  between operations  14.5 us (4%)
  local copies, waits for them, and re-layouts  8.1 us (2%)
    all_gather x1, waiting for transfers between devices, body(): lax.all_gather(up_weight, 'dp', axis=1, tiled=True)  44.9 us
    psum x1, blocking collectives, body(): gain_sum = lax.psum(grad_gain, ('dp', 'expert'))  44.7 us
    all_gather x1, waiting for transfers between devices, body(): lax.all_gather(gate_weight, 'dp', axis=1, tiled=True)  44.6 us
    psum x1, blocking collectives, body(): router_mine = lax.psum(router_part, 'expert').astype(jnp.float32)  17.1 us
    all_gather x1, blocking collectives, body(): router_full = lax.all_gather(router_weight, 'dp', axis=0, tiled=True)  16.8 us
    all_gather x1, waiting for transfers between devices, body(): lax.all_gather(active, 'dp', axis=0, tiled=True)  14.1 us
    all_to_all x1, waiting for transfers between devices, body(): lax.all_to_all(flat_rows, 'dp', split_axis=1, concat_axis=0, tiled=True)  13.1 us
    all_gather x1, waiting for transfers between devices, body(): lax.all_gather(down_weight, 'dp', axis=1, tiled=True)  9.29 us
  transfers between devices with their start and end apart: 13, of which 8 were waited for; matrix products, arithmetic and copies ran while one was open for 12% of the time, Pallas kernels for 0%

commit v1 on v0

--- a/solution.py
+++ b/solution.py
@@ -29,7 +29,11 @@
 def pick_matrix(expert_ids, window, capacity):
     flat_ids = expert_ids.reshape(-1)
     chosen = (flat_ids[:, None] == jnp.arange(window, dtype=jnp.int32)[None, :]).astype(jnp.int32)
-    before = jnp.cumsum(chosen, axis=0, dtype=jnp.int32) - chosen
+    order = jnp.arange(flat_ids.shape[0], dtype=jnp.int32)
+    earlier = (order[None, :] < order[:, None]).astype(jnp.bfloat16)
+    before = jnp.dot(
+        earlier, chosen.astype(jnp.bfloat16), preferred_element_type=jnp.float32
+    ).astype(jnp.int32)
     position = jnp.sum(before * chosen, axis=-1)
     target = jnp.where(flat_ids < window, flat_ids * capacity + position, -1)
     columns = jnp.arange(window * capacity, dtype=jnp.int32)

time: 341 us -> 341 us (level)
  transfers between devices with their start and end apart: 13 -> 13, of which waited for: 8 -> 8; matrix products, arithmetic and copies ran while one was open for 12% -> 11% of each run, Pallas kernels for 0% -> 0%
where the time goes in v1:
time: 341 us; the launch traced here: 340 us
  waiting for transfers between devices  150 us (44%)
  blocking collectives  78.4 us (23%)
  matrix products  47.6 us (14%)
  starting transfers between devices  22 us (6%)
  other arithmetic  19.3 us (6%)
  between operations  14.4 us (4%)
  local copies, waits for them, and re-layouts  8.3 us (2%)
    all_gather x1, waiting for transfers between devices, body(): lax.all_gather(up_weight, 'dp', axis=1, tiled=True)  44.9 us
    psum x1, blocking collectives, body(): gain_sum = lax.psum(grad_gain, ('dp', 'expert'))  44.6 us
    all_gather x1, waiting for transfers between devices, body(): lax.all_gather(gate_weight, 'dp', axis=1, tiled=True)  44.6 us
    psum x1, blocking collectives, body(): router_mine = lax.psum(router_part, 'expert').astype(jnp.float32)  17.1 us
    all_gather x1, blocking collectives, body(): router_full = lax.all_gather(router_weight, 'dp', axis=0, tiled=True)  16.7 us
    all_gather x1, waiting for transfers between devices, body(): lax.all_gather(active, 'dp', axis=0, tiled=True)  14.1 us
    all_to_all x1, waiting for transfers between devices, body(): lax.all_to_all(flat_rows, 'dp', split_axis=1, concat_axis=0, tiled=True)  13.1 us
    all_gather x1, waiting for transfers between devices, body(): lax.all_gather(down_weight, 'dp', axis=1, tiled=True)  10.7 us
  transfers between devices with their start and end apart: 13, of which 8 were waited for; matrix products, arithmetic and copies ran while one was open for 11% of the time, Pallas kernels for 0%

profile of v1, /device:TPU:0, one launch (start us, length us, event | category | flops | bytes accessed | tf_op | source)
XLA Modules:
  0.0 339.8 jit_solution(12409218663453684300)
XLA Ops:
  11.8 16.7 %all_gather.21 = bf16[2048,64]{0,1:T(8,128)(2,1)S(1)} all-gather(bf16[256,64]{0,1:T(8,128)(2,1)} %param.10), channel_id=1, replica_groups=mesh['dp'=8,'expert'=4] {'dp'}, dimensions={0}, use_global_device_ids=true | all-gather | bytes 294912 | tf_op jit(solution)/shard_map/all_gather | solution.py:84
  34.0 3.8 %all-to-all-start.2 = ((bf16[4,32,2048]{2,1,0:T(8,128)(2,1)}), bf16[4,32,2048]{2,1,0:T(8,128)(2,1)S(1)}, u32[]{:S(2)}, u32[]{:S(2)}) async-start(bf16[4,32,2048]{2,1,0:T(8,128)(2,1)} %bitcast.10), calls=%async_computation.2 | async-start | bytes 1048576 | tf_op jit(solution)/shard_map/all_to_all | solution.py:126
  39.3 7.1 %all-to-all-done.2 = bf16[4,32,2048]{2,1,0:T(8,128)(2,1)S(1)} async-done(((bf16[4,32,2048]{2,1,0:T(8,128)(2,1)}), bf16[4,32,2048]{2,1,0:T(8,128)(2,1)S(1)}, u32[]{:S(2)}, u32[]{:S(2)}) %all-to-all-start.2) | async-done | bytes 524320 | tf_op jit(solution)/shard_map/all_to_all | solution.py:126
  46.4 3.5 %all-to-all-start = ((bf16[4,32,2048]{2,1,0:T(8,128)(2,1)}), bf16[4,32,2048]{2,1,0:T(8,128)(2,1)S(1)}, u32[]{:S(2)}, u32[]{:S(2)}) async-start(bf16[4,32,2048]{2,1,0:T(8,128)(2,1)} %bitcast.3), calls=%async_computation | async-start | bytes 1048576 | tf_op jit(solution)/shard_map/all_to_all | solution.py:105
  49.9 10.7 %all-gather.11.cloned.1.call-done = bf16[1,2048,1024]{2,1,0:T(8,128)(2,1)} async-done(((bf16[1,256,1024]{2,1,0:T(8,128)(2,1)}), bf16[1,2048,1024]{2,1,0:T(8,128)(2,1)}) %all-gather.11.cloned.1.call-update) | async-done | bytes 4194320 | tf_op jit(solution)/shard_map/all_gather | solution.py:100
  63.5 44.9 %all-gather.9.cloned.1.call-done = bf16[1,2048,1024]{2,1,0:T(8,128)(2,1)} async-done(((bf16[1,256,1024]{2,1,0:T(8,128)(2,1)}), bf16[1,2048,1024]{2,1,0:T(8,128)(2,1)}) %all-gather.9.cloned.1.call-update) | async-done | bytes 4194320 | tf_op jit(solution)/shard_map/all_gather | solution.py:99
  111.3 44.6 %all-gather.7.cloned.1.call-done = bf16[1,2048,1024]{2,1,0:T(8,128)(2,1)} async-done(((bf16[1,256,1024]{2,1,0:T(8,128)(2,1)}), bf16[1,2048,1024]{2,1,0:T(8,128)(2,1)}) %all-gather.7.cloned.1.call-update) | async-done | bytes 4194320 | tf_op jit(solution)/shard_map/all_gather | solution.py:98
  155.9 4.0 %multiply_convert_fusion.1 = (bf16[128,1024]{1,0:T(8,128)(2,1)}, bf16[128,1024]{1,0:T(8,128)(2,1)S(1)}, bf16[128,1024]{1,0:T(8,128)(2,1)}) fusion(f32[128,1024]{1,0:T(8,128)S(1)} %fusion, f32[128,1024]{1,0:T(8,128)S(1)} %fusion.6, bf16[128,2048]{1,0:T(8,128)(2,1)S(1)} %bitcast.98, bf16[1,2048,1024]{2,1,0:T(8,128)(2,1)} %all-gather.7.cloned.1.call-done), kind=kOutput, calls=%fused_computation.50 | convolution fusion | flops 538968064 | bytes 6553600 | tf_op jit(solution)/shard_map/dot_general | solution.py:45
  159.9 4.6 %fusion.19 = bf16[128,2048]{1,0:T(8,128)(2,1)} fusion(bf16[128,1024]{1,0:T(8,128)(2,1)S(1)} %get-tuple-element.13, bf16[1,2048,1024]{2,1,0:T(8,128)(2,1)} %all-gather.11.cloned.1.call-done), kind=kOutput, calls=%fused_computation.22 | convolution fusion | flops 537133056 | bytes 4980736 | tf_op jit(solution)/shard_map/dot_general | solution.py:48
  164.5 3.6 %all-to-all-start.1 = ((bf16[4,32,2048]{2,1,0:T(8,128)(2,1)}), bf16[4,32,2048]{2,1,0:T(8,128)(2,1)S(1)}, u32[]{:S(2)}, u32[]{:S(2)}) async-start(bf16[4,32,2048]{2,1,0:T(8,128)(2,1)} %bitcast.8), calls=%async_computation.1 | async-start | bytes 1048576 | tf_op jit(solution)/shard_map/all_to_all | solution.py:112
  168.2 8.5 %all-to-all-done.1 = bf16[4,32,2048]{2,1,0:T(8,128)(2,1)S(1)} async-done(((bf16[4,32,2048]{2,1,0:T(8,128)(2,1)}), bf16[4,32,2048]{2,1,0:T(8,128)(2,1)S(1)}, u32[]{:S(2)}, u32[]{:S(2)}) %all-to-all-start.1) | async-done | bytes 524320 | tf_op jit(solution)/shard_map/all_to_all | solution.py:112
  177.1 5.1 %fusion.36 = f32[1,128,8]{2,0,1:T(1,128)} fusion(s32[128,8]{1,0:T(8,128)} %copy-done.9, f32[128]{0:T(128)S(1)} %fusion.24), kind=kOutput, calls=%fused_computation.55 | convolution fusion | flops 1703936 | bytes 8704 | tf_op jit(solution)/shard_map/tks,s->tk/dot_general | solution.py:119
  186.4 3.9 %fusion.4 = f32[128,2048]{1,0:T(8,128)S(1)} fusion(bf16[128,1024]{1,0:T(8,128)(2,1)S(1)} %copy-done.8, bf16[1,2048,1024]{2,1,0:T(8,128)(2,1)} %all-gather.9.cloned.1.call-done), kind=kOutput, calls=%fused_computation.5 | convolution fusion | flops 536870912 | bytes 5505024 | tf_op jit(solution)/shard_map/dot_general | solution.py:62
  192.6 3.6 %all-to-all-start.3 = ((bf16[4,32,2048]{2,1,0:T(8,128)(2,1)}), bf16[4,32,2048]{2,1,0:T(8,128)(2,1)S(1)}, u32[]{:S(2)}, u32[]{:S(2)}) async-start(bf16[4,32,2048]{2,1,0:T(8,128)(2,1)} %bitcast.103), calls=%async_computation.3 | async-start | bytes 1048576 | tf_op jit(solution)/shard_map/all_to_all | solution.py:132
  203.8 3.5 %all-to-all-start.4 = ((bf16[128,8,256]{0,2,1:T(8,128)(2,1)}), bf16[128,8,256]{0,2,1:T(8,128)(2,1)S(1)}, u32[]{:S(2)}, u32[]{:S(2)}) async-start(bf16[128,8,256]{0,2,1:T(8,128)(2,1)} %copy.39), calls=%async_computation.5 | async-start | bytes 1048576 | tf_op jit(solution)/shard_map/all_to_all | solution.py:137
  209.6 13.1 %all-to-all-done.4 = bf16[128,8,256]{0,2,1:T(8,128)(2,1)S(1)} async-done(((bf16[128,8,256]{0,2,1:T(8,128)(2,1)}), bf16[128,8,256]{0,2,1:T(8,128)(2,1)S(1)}, u32[]{:S(2)}, u32[]{:S(2)}) %all-to-all-start.4) | async-done | bytes 524320 | tf_op jit(solution)/shard_map/all_to_all | solution.py:137
  222.7 3.5 %all-to-all-start.5 = ((bf16[128,8,256]{0,2,1:T(8,128)(2,1)}), bf16[128,8,256]{0,2,1:T(8,128)(2,1)S(1)}, u32[]{:S(2)}, u32[]{:S(2)}) async-start(bf16[128,8,256]{0,2,1:T(8,128)(2,1)} %copy.40), calls=%async_computation.6 | async-start | bytes 1048576 | tf_op jit(solution)/shard_map/all_to_all | solution.py:138
  227.6 44.6 %psum.14 = f32[2048]{0:T(1024)} all-reduce(f32[2048]{0:T(1024)S(1)} %get-tuple-element.7), channel_id=1, replica_groups=mesh['dp'=8,'expert'=4] {'dp','expert'}, use_global_device_ids=true, to_apply=%region_10.11 | all-reduce | flops 2048 | bytes 16384 | tf_op jit(solution)/shard_map/psum | solution.py:165
  272.2 17.1 %psum.15 = bf16[256,64]{0,1:T(8,128)(2,1)S(1)} all-reduce(bf16[256,64]{0,1:T(8,128)(2,1)} %reduce-scatter.2.cloned.1.call-done), channel_id=1, replica_groups=mesh['dp'=8,'expert'=4] {'expert'}, use_global_device_ids=true, to_apply=%region_12.13 | all-reduce | flops 16384 | bytes 65536 | tf_op jit(solution)/shard_map/psum | solution.py:164
  289.9 4.8 %convolution_convert_fusion.1 = bf16[8,256,1024]{2,1,0:T(8,128)(2,1)} fusion(bf16[8,128,1024]{2,1,0:T(8,128)(2,1)} %bitcast.104, bf16[128,8,256]{0,2,1:T(8,128)(2,1)S(1)} %all-to-all-done.4), kind=kOutput, calls=%fused_computation.16 | convolution fusion | flops 538968064 | bytes 6815744 | tf_op jit(solution)/shard_map/krd,krf->kdf/dot_general | solution.py:69
  294.8 4.8 %convolution_convert_fusion.2 = bf16[8,256,1024]{2,1,0:T(8,128)(2,1)} fusion(bf16[8,128,1024]{2,1,0:T(8,128)(2,1)} %bitcast.106, bf16[128,8,256]{0,2,1:T(8,128)(2,1)S(1)} %all-to-all-done.4), kind=kOutput, calls=%fused_computation.17 | convolution fusion | flops 538968064 | bytes 6815744 | tf_op jit(solution)/shard_map/krd,krf->kdf/dot_general | solution.py:68
  299.5 14.1 %all-gather.17.cloned.1.call-done = bf16[1024,1024]{1,0:T(8,128)(2,1)} async-done(((bf16[128,1024]{1,0:T(8,128)(2,1)}), bf16[1024,1024]{1,0:T(8,128)(2,1)}) %all-gather.17.cloned.1.call-update) | async-done | bytes 2097168 | tf_op jit(solution)/shard_map/all_gather | solution.py:144
  316.6 7.9 %pad_maximum_fusion = bf16[8,256,3072]{2,1,0:T(8,128)(2,1)} fusion(bf16[8,256,1024]{2,1,0:T(8,128)(2,1)S(1)} %convolution_convert_fusion, bf16[8,256,1024]{2,1,0:T(8,128)(2,1)S(1)} %copy-done.1, bf16[8,256,1024]{2,1,0:T(8,128)(2,1)} %convolution_convert_fusion.2), kind=kLoop, calls=%fused_computation | loop fusion | flops 37748736 | bytes 25165824 | tf_op jit(solution)/shard_map/concatenate | solution.py:73
  324.5 7.3 %reduce = bf16[256,3072]{1,0:T(8,128)(2,1)S(1)} reduce(bf16[8,256,3072]{2,1,0:T(8,128)(2,1)} %pad_maximum_fusion, bf16[]{:T(256)} %constant.27), dimensions={0}, to_apply=%region_13.14.clone | reduce | flops 5505024 | bytes 14155778 | tf_op jit(solution)/shard_map/reduce_sum | solution.py:75
  (89 shorter events, 40.1 us)
Async XLA Ops:
  7.2 25.4 %copy-start = (bf16[128,2048]{1,0:T(8,128)(2,1)S(1)}, bf16[128,2048]{1,0:T(8,128)(2,1)}, u32[]{:S(2)}) copy-start(bf16[128,2048]{1,0:T(8,128)(2,1)} %param.15) | copy-start | bytes 1572868
  7.2 24.6 %copy-start.11 = (s32[128,8]{0,1:T(8,128)S(1)}, s32[128,8]{0,1:T(8,128)}, u32[]{:S(2)}) copy-start(s32[128,8]{0,1:T(8,128)} %param.11) | copy-start | bytes 12292
  7.2 30.9 %copy-start.2 = (bf16[128,2048]{1,0:T(8,128)(2,1)S(1)}, bf16[128,2048]{1,0:T(8,128)(2,1)}, u32[]{:S(2)}) copy-start(bf16[128,2048]{1,0:T(8,128)(2,1)} %param.8) | copy-start | bytes 1572868
  7.2 30.9 %copy-start.10 = (f32[2048]{0:T(1024)S(1)}, f32[2048]{0:T(1024)}, u32[]{:S(2)}) copy-start(f32[2048]{0:T(1024)} %param.9) | copy-start | bytes 24580
  7.2 53.4 %all-gather.11.cloned.1.call-start = ((), (), s32[]{:S(2)}) async-start(), calls=%async_computation.9 | async-start | bytes 4718592 | tf_op jit(solution)/shard_map/all_gather | solution.py:100
  8.0 100.5 %all-gather.9.cloned.1.call-start = ((), (), s32[]{:S(2)}) async-start(), calls=%async_computation.8 | async-start | bytes 4718592 | tf_op jit(solution)/shard_map/all_gather | solution.py:99
  8.7 147.2 %all-gather.7.cloned.1.call-start = ((), (), s32[]{:S(2)}) async-start(), calls=%async_computation.7 | async-start | bytes 4718592 | tf_op jit(solution)/shard_map/all_gather | solution.py:98
  11.8 34.6 %copy-start.9 = (s32[128,8]{1,0:T(8,128)}, s32[128,8]{1,0:T(8,128)S(1)}, u32[]{:S(2)}) copy-start(s32[128,8]{1,0:T(8,128)S(1)} %copy.38) | copy-start | bytes 12292
  34.0 12.4 %all-to-all-start.2 = ((bf16[4,32,2048]{2,1,0:T(8,128)(2,1)}), bf16[4,32,2048]{2,1,0:T(8,128)(2,1)S(1)}, u32[]{:S(2)}, u32[]{:S(2)}) async-start(bf16[4,32,2048]{2,1,0:T(8,128)(2,1)} %bitcast.10), calls=%async_computation.2 | async-start | bytes 1048576 | tf_op jit(solution)/shard_map/all_to_all | solution.py:126
  46.4 17.1 %all-to-all-start = ((bf16[4,32,2048]{2,1,0:T(8,128)(2,1)}), bf16[4,32,2048]{2,1,0:T(8,128)(2,1)S(1)}, u32[]{:S(2)}, u32[]{:S(2)}) async-start(bf16[4,32,2048]{2,1,0:T(8,128)(2,1)} %bitcast.3), calls=%async_computation | async-start | bytes 1048576 | tf_op jit(solution)/shard_map/all_to_all | solution.py:105
  159.9 24.5 %copy-start.4 = (bf16[128,1024]{1,0:T(8,128)(2,1)}, bf16[128,1024]{1,0:T(8,128)(2,1)S(1)}, u32[]{:S(2)}) copy-start(bf16[128,1024]{1,0:T(8,128)(2,1)S(1)} %get-tuple-element.13) | copy-start | bytes 786436
  159.9 26.4 %copy-start.8 = (bf16[128,1024]{1,0:T(8,128)(2,1)S(1)}, bf16[128,1024]{1,0:T(8,128)(2,1)}, u32[]{:S(2)}) copy-start(bf16[128,1024]{1,0:T(8,128)(2,1)} %get-tuple-element.14) | copy-start | bytes 786436
  164.5 12.1 %all-to-all-start.1 = ((bf16[4,32,2048]{2,1,0:T(8,128)(2,1)}), bf16[4,32,2048]{2,1,0:T(8,128)(2,1)S(1)}, u32[]{:S(2)}, u32[]{:S(2)}) async-start(bf16[4,32,2048]{2,1,0:T(8,128)(2,1)} %bitcast.8), calls=%async_computation.1 | async-start | bytes 1048576 | tf_op jit(solution)/shard_map/all_to_all | solution.py:112
  168.2 104.0 %reduce-scatter.2.cloned.1.call-start = ((), (), s32[]{:S(2)}) async-start(), calls=%async_computation.10 | async-start | bytes 294912 | tf_op jit(solution)/shard_map/reduce_scatter | solution.py:161
  177.1 13.2 %copy-start.5 = (bf16[128,1024]{1,0:T(8,128)(2,1)S(1)}, bf16[128,1024]{1,0:T(8,128)(2,1)}, u32[]{:S(2)}) copy-start(bf16[128,1024]{1,0:T(8,128)(2,1)} %get-tuple-element.12) | copy-start | bytes 786436
  184.5 105.5 %all-gather.15.cloned.1.call-start = ((), (), s32[]{:S(2)}) async-start(), calls=%async_computation.12 | async-start | bytes 2359296 | tf_op jit(solution)/shard_map/all_gather | solution.py:143
  185.0 109.7 %all-gather.13.cloned.1.call-start = ((), (), s32[]{:S(2)}) async-start(), calls=%async_computation.11 | async-start | bytes 2359296 | tf_op jit(solution)/shard_map/all_gather | solution.py:142
  185.6 128.0 %all-gather.17.cloned.1.call-start = ((), (), s32[]{:S(2)}) async-start(), calls=%async_computation.13 | async-start | bytes 2359296 | tf_op jit(solution)/shard_map/all_gather | solution.py:144
  186.4 3.9 %copy-start.3 = (bf16[1,2048,1024]{2,1,0:T(8,128)(2,1)S(1)}, bf16[1,2048,1024]{2,1,0:T(8,128)(2,1)}, u32[]{:S(2)}) copy-start(bf16[1,2048,1024]{2,1,0:T(8,128)(2,1)} %all-gather.7.cloned.1.call-done) | copy-start | bytes 12582916
  192.6 15.0 %copy-start.7 = (bf16[2048,64]{0,1:T(8,128)(2,1)S(1)}, bf16[2048,64]{0,1:T(8,128)(2,1)}, u32[]{:S(2)}) copy-start(bf16[2048,64]{0,1:T(8,128)(2,1)} %copy-done.6) | copy-start | bytes 786436
  192.6 11.2 %all-to-all-start.3 = ((bf16[4,32,2048]{2,1,0:T(8,128)(2,1)}), bf16[4,32,2048]{2,1,0:T(8,128)(2,1)S(1)}, u32[]{:S(2)}, u32[]{:S(2)}) async-start(bf16[4,32,2048]{2,1,0:T(8,128)(2,1)} %bitcast.103), calls=%async_computation.3 | async-start | bytes 1048576 | tf_op jit(solution)/shard_map/all_to_all | solution.py:132
  197.1 11.4 %copy-start.13 = (f32[128]{0:T(128)S(1)}, f32[128]{0:T(128)}, u32[]{:S(2)}) copy-start(f32[128]{0:T(128)} %copy-done.12) | copy-start | bytes 1540
  203.8 18.9 %all-to-all-start.4 = ((bf16[128,8,256]{0,2,1:T(8,128)(2,1)}), bf16[128,8,256]{0,2,1:T(8,128)(2,1)S(1)}, u32[]{:S(2)}, u32[]{:S(2)}) async-start(bf16[128,8,256]{0,2,1:T(8,128)(2,1)} %copy.39), calls=%async_computation.5 | async-start | bytes 1048576 | tf_op jit(solution)/shard_map/all_to_all | solution.py:137
  222.7 76.8 %all-to-all-start.5 = ((bf16[128,8,256]{0,2,1:T(8,128)(2,1)}), bf16[128,8,256]{0,2,1:T(8,128)(2,1)S(1)}, u32[]{:S(2)}, u32[]{:S(2)}) async-start(bf16[128,8,256]{0,2,1:T(8,128)(2,1)} %copy.40), calls=%async_computation.6 | async-start | bytes 1048576 | tf_op jit(solution)/shard_map/all_to_all | solution.py:138
  (3 other events, 5.4 us)
Sparse Core Ops, SparseCore 0:
  9.7 50.8 all-gather.10
  62.2 46.1 all-gather.8
  110.0 45.8 all-gather.6
  184.6 28.2 reduce-scatter.1
  214.4 38.7 all-gather.14
  254.8 28.5 all-gather.12
  285.0 28.5 all-gather.16

commit v2 on v1

v2 whole, which is shorter than its diff:
```python
import jax
import jax.numpy as jnp
from jax import lax
from jax.sharding import PartitionSpec as P

D = 2048
FF = 1024
CAP = 32


EPSILON = 1e-05
HIGHEST = lax.Precision.HIGHEST


def normalize(inputs, norm_gain):
    meansq = jnp.mean(inputs * inputs, axis=-1, keepdims=True)
    return inputs * lax.rsqrt(meansq + EPSILON) * norm_gain


def gate_weights(logits, expert_ids):
    member = (
        expert_ids[:, :, None] == jnp.arange(logits.shape[-1], dtype=jnp.int32)[None, None, :]
    ).astype(jnp.float32)
    picked = jnp.sum(member * logits[:, None, :], axis=-1)
    raised = jnp.exp(picked)
    return raised / jnp.sum(raised, axis=-1, keepdims=True)


def pick_matrix(expert_ids, window, capacity):
    flat_ids = expert_ids.reshape(-1)
    chosen = (flat_ids[:, None] == jnp.arange(window, dtype=jnp.int32)[None, :]).astype(jnp.int32)
    order = jnp.arange(flat_ids.shape[0], dtype=jnp.int32)
    earlier = (order[None, :] < order[:, None]).astype(jnp.bfloat16)
    before = jnp.dot(
        earlier, chosen.astype(jnp.bfloat16), preferred_element_type=jnp.float32
    ).astype(jnp.int32)
    position = jnp.sum(before * chosen, axis=-1)
    target = jnp.where(flat_ids < window, flat_ids * capacity + position, -1)
    columns = jnp.arange(window * capacity, dtype=jnp.int32)
    matrix = (target[:, None] == columns[None, :]).astype(jnp.float32)
    return matrix.reshape(expert_ids.shape[0], expert_ids.shape[1], window * capacity)


def small_gather(values, axis):
    count = lax.axis_size(axis)
    copies = jnp.broadcast_to(values[None], (count,) + values.shape)
    return lax.all_to_all(copies, axis, split_axis=0, concat_axis=0, tiled=True)


def expert_pass(slot_rows, slot_grads, w_gate, w_up, w_down):
    gate_pre = jnp.dot(slot_rows, w_gate, preferred_element_type=jnp.float32)
    up_pre = jnp.dot(slot_rows, w_up, preferred_element_type=jnp.float32)
    sigmoid_gate = jax.nn.sigmoid(gate_pre)
    active = (gate_pre * sigmoid_gate * up_pre).astype(jnp.bfloat16)
    back = jnp.dot(slot_grads, w_down, preferred_element_type=jnp.float32)
    grad_gate = (back * up_pre * sigmoid_gate * (1.0 + gate_pre * (1.0 - sigmoid_gate))).astype(
        jnp.bfloat16
    )
    grad_upper = (back * gate_pre * sigmoid_gate).astype(jnp.bfloat16)
    return (active, grad_gate, grad_upper)


def body(
    tokens, norm_gain, router_weight, expert_ids, gate_weight, up_weight, down_weight, cotangent
):
    window = lax.axis_size("expert")
    groups_dp = lax.axis_size("dp")
    slot_count = window * CAP
    shard_rows = D // groups_dp
    w_gate = lax.all_gather(gate_weight[0], "dp", axis=0, tiled=True)
    w_up = lax.all_gather(up_weight[0], "dp", axis=0, tiled=True)
    w_down = lax.all_gather(down_weight[0], "dp", axis=0, tiled=True)
    router_full = small_gather(router_weight, "dp").reshape(D, router_weight.shape[1])
    inputs = tokens.astype(jnp.float32)
    hidden = normalize(inputs, norm_gain).astype(jnp.bfloat16)
    logits = jnp.dot(hidden, router_full, preferred_element_type=jnp.float32)
    weights, gate_back = jax.vjp(lambda values: gate_weights(values, expert_ids), logits)
    pick_table = pick_matrix(expert_ids, window, CAP)
    spread_half = jnp.sum(pick_table, axis=1).astype(jnp.bfloat16)
    blending = jnp.sum(pick_table * weights[:, :, None], axis=1)
    outgoing = jnp.dot(spread_half.T, hidden, preferred_element_type=jnp.float32).astype(
        jnp.bfloat16
    )
    outgoing_grad = jnp.dot(
        blending.T, cotangent.astype(jnp.float32), precision=HIGHEST
    ).astype(jnp.bfloat16)
    leaving = jnp.stack(
        [outgoing.reshape(window, CAP, D), outgoing_grad.reshape(window, CAP, D)], axis=1
    )
    arrived = lax.all_to_all(leaving, "expert", split_axis=0, concat_axis=0, tiled=True)
    flat_rows = arrived[:, 0].reshape(slot_count, D)
    flat_grads = arrived[:, 1].reshape(slot_count, D)
    cut = jnp.stack([flat_rows, flat_grads]).reshape(2, slot_count, groups_dp, shard_rows)
    cut = lax.all_to_all(
        cut.transpose(2, 0, 1, 3), "dp", split_axis=0, concat_axis=0, tiled=True
    )
    rows_cut = cut[:, 0].reshape(groups_dp * slot_count, shard_rows)
    grads_cut = cut[:, 1].reshape(groups_dp * slot_count, shard_rows)
    active, grad_gate, grad_upper = expert_pass(flat_rows, flat_grads, w_gate, w_up, w_down)
    units = lax.all_gather(
        jnp.concatenate([grad_gate, grad_upper, active], axis=1), "dp", axis=0, tiled=True
    )
    output = jnp.dot(active, w_down.T, preferred_element_type=jnp.float32).astype(jnp.bfloat16)
    grad_rows = jnp.dot(grad_gate, w_gate.T, preferred_element_type=jnp.float32)
    grad_rows = (
        grad_rows + jnp.dot(grad_upper, w_up.T, preferred_element_type=jnp.float32)
    ).astype(jnp.bfloat16)
    produced = jnp.stack(
        [output.reshape(window, CAP, D), grad_rows.reshape(window, CAP, D)], axis=1
    )
    came_back = lax.all_to_all(produced, "expert", split_axis=0, concat_axis=0, tiled=True)
    returned = came_back[:, 0].reshape(slot_count, D)
    grad_back = came_back[:, 1].reshape(slot_count, D)
    returned_wide = returned.astype(jnp.float32)
    mixed_out = jnp.dot(blending, returned_wide, precision=HIGHEST).astype(jnp.bfloat16)
    gathered_cot = jnp.dot(spread_half.T, cotangent, preferred_element_type=jnp.float32)
    per_slot = jnp.sum(gathered_cot * returned_wide, axis=-1)
    grad_weights = jnp.sum(pick_table * per_slot[None, None, :], axis=-1)
    grad_logits = gate_back(grad_weights)[0]
    grad_router = jnp.dot(hidden.astype(jnp.float32).T, grad_logits, precision=HIGHEST)
    router_parts = lax.all_to_all(
        grad_router.astype(jnp.bfloat16).reshape(groups_dp, shard_rows, -1),
        "dp",
        split_axis=0,
        concat_axis=0,
        tiled=True,
    )
    router_part = jnp.sum(router_parts.astype(jnp.float32), axis=0)
    router_mine = jnp.sum(small_gather(router_part, "expert"), axis=0)
    grad_hidden = jnp.dot(spread_half, grad_back, preferred_element_type=jnp.float32)
    grad_hidden = grad_hidden + jnp.dot(
        grad_logits, router_full.astype(jnp.float32).T, precision=HIGHEST
    )
    unused_value, norm_back = jax.vjp(normalize, inputs, norm_gain)
    grad_inputs, grad_gain = norm_back(grad_hidden)
    gain_sum = jnp.sum(small_gather(grad_gain, ("dp", "expert")), axis=0)
    grad_rows_pair = lax.dot_general(
        rows_cut,
        units[:, : 2 * FF],
        (((0,), (0,)), ((), ())),
        preferred_element_type=jnp.float32,
    ).astype(jnp.bfloat16)
    grad_down = lax.dot_general(
        grads_cut,
        units[:, 2 * FF :],
        (((0,), (0,)), ((), ())),
        preferred_element_type=jnp.float32,
    ).astype(jnp.bfloat16)
    return (
        mixed_out,
        grad_inputs.astype(jnp.bfloat16),
        gain_sum,
        router_mine,
        grad_rows_pair[:, :FF][None],
        grad_rows_pair[:, FF:][None],
        grad_down[None],
    )


def solution(mesh):
    in_specs = (
        P(("dp", "expert"), None),
        P(),
        P("dp", None),
        P(("dp", "expert"), None),
        P("expert", "dp", None),
        P("expert", "dp", None),
        P("expert", "dp", None),
        P(("dp", "expert"), None),
    )
    out_specs = (
        P(("dp", "expert"), None),
        P(("dp", "expert"), None),
        P(),
        P("dp", None),
        P("expert", "dp", None),
        P("expert", "dp", None),
        P("expert", "dp", None),
    )
    return jax.shard_map(body, mesh=mesh, in_specs=in_specs, out_specs=out_specs, check_vma=False)
```

time: 341 us -> 297 us (0.87)
  blocking collectives: 78.4 us -> 15.5 us
  waiting for transfers between devices: 150 us -> 186 us
  matrix products: 47.6 us -> 35.1 us
  other arithmetic: 19.3 us -> 9.71 us
  starting transfers between devices: 22 us -> 26.4 us
    psum x2 -> x0, blocking collectives: 61.7 us -> none  [the longest x1 44.6 us: body(): gain_sum = lax.psum(grad_gain, ('dp', 'expert'))]
    all_to_all x5, waiting for transfers between devices: 23.3 us -> 74.4 us  [the longest x1 43.4 us: body(): lax.all_to_all(cut.transpose(2, 0, 1, 3), 'dp', split_axis=0, concat_axis...]
    all_gather x1 -> x0, blocking collectives: 16.7 us -> none  [body(): router_full = lax.all_gather(router_weight, 'dp', axis=0, tiled=True)]
    all_to_all x0 -> x1, blocking collectives: none -> 15.5 us  [body(): lax.all_to_all(leaving, 'expert', split_axis=0, concat_axis=0, tiled=True)]
    all_gather x6 -> x4, waiting for transfers between devices: 114 us -> 101 us  [the longest x1 44 us: body(): w_down = lax.all_gather(down_weight[0], 'dp', axis=0, tiled=True)]
    dot_general x11 -> x8, matrix products: 38.9 us -> 27 us  [the longest x1 4.18 us: body(): jnp.dot(active, w_down.T, preferred_element_type=jnp.float32)]
    concatenate x1, other arithmetic: 7.89 us -> 0.94 us  [body(): jnp.concatenate([grad_gate, grad_upper, active], axis=1)]
    reduce_sum x1 -> x4, other arithmetic: 7.25 us -> 1.81 us  [the longest x1 0.76 us: body(): gain_sum = jnp.sum(small_gather(grad_gain, ('dp', 'expert')), axis=0)]
  transfers between devices with their start and end apart: 13 -> 10, of which waited for: 8 -> 9; matrix products, arithmetic and copies ran while one was open for 11% -> 14% of each run, Pallas kernels for 0% -> 0%
where the time goes in v2:
time: 297 us; the launch traced here: 296 us
  waiting for transfers between devices  186 us (63%)
  matrix products  35.1 us (12%)
  starting transfers between devices  26.4 us (9%)
  blocking collectives  15.5 us (5%)
  between operations  14.1 us (5%)
  other arithmetic  9.71 us (3%)
  local copies, waits for them, and re-layouts  9.28 us (3%)
    all_gather x1, waiting for transfers between devices, body(): w_down = lax.all_gather(down_weight[0], 'dp', axis=0, tiled=True)  44 us
    all_gather x1, waiting for transfers between devices, body(): w_up = lax.all_gather(up_weight[0], 'dp', axis=0, tiled=True)  43.8 us
    all_to_all x1, waiting for transfers between devices, body(): lax.all_to_all(cut.transpose(2, 0, 1, 3), 'dp', split_axis=0, concat_axis...  43.4 us
    all_to_all x3, waiting for transfers between devices, small_gather(): return lax.all_to_all(copies, axis, split_axis=0, concat_axis=0, tiled=True)  23.9 us
    all_to_all x1, blocking collectives, body(): lax.all_to_all(leaving, 'expert', split_axis=0, concat_axis=0, tiled=True)  15.5 us
    all_gather x1, waiting for transfers between devices, body(): w_gate = lax.all_gather(gate_weight[0], 'dp', axis=0, tiled=True)  13.1 us
    all_to_all x3, starting transfers between devices, small_gather(): return lax.all_to_all(copies, axis, split_axis=0, concat_axis=0, tiled=True)  12.5 us
    all_to_all x1, waiting for transfers between devices, body(): lax.all_to_all(produced, 'expert', split_axis=0, concat_axis=0, tiled=True)  8.45 us
  transfers between devices with their start and end apart: 10, of which 9 were waited for; matrix products, arithmetic and copies ran while one was open for 14% of the time, Pallas kernels for 0%

profile of v2, /device:TPU:0, one launch (start us, length us, event | category | flops | bytes accessed | tf_op | source)
XLA Modules:
  0.0 295.9 jit_solution(14810518676882303216)
XLA Ops:
  10.9 6.3 %all-to-all-start = ((bf16[8,256,64]{1,2,0:T(8,128)(2,1)}), bf16[8,256,64]{1,2,0:T(8,128)(2,1)S(1)}, u32[]{:S(2)}, u32[]{:S(2)}) async-start(bf16[8,256,64]{1,2,0:T(8,128)(2,1)} %broadcast_in_dim.25), calls=%async_computation | async-start | bytes 524288 | tf_op jit(solution)/shard_map/all_to_all | solution.py:47
  19.8 11.5 %all-to-all-done = bf16[8,256,64]{1,2,0:T(8,128)(2,1)S(1)} async-done(((bf16[8,256,64]{1,2,0:T(8,128)(2,1)}), bf16[8,256,64]{1,2,0:T(8,128)(2,1)S(1)}, u32[]{:S(2)}, u32[]{:S(2)}) %all-to-all-start) | async-done | bytes 262176 | tf_op jit(solution)/shard_map/all_to_all | solution.py:47
  34.0 15.5 %all_to_all.36 = bf16[4,2,32,2048]{3,2,1,0:T(8,128)(2,1)S(1)} all-to-all(bf16[4,2,32,2048]{3,2,1,0:T(8,128)(2,1)S(1)} %pad_maximum_fusion), channel_id=1, replica_groups=mesh['dp'=8,'expert'=4] {'expert'}, dimensions={0} | all-to-all | bytes 2097152 | tf_op jit(solution)/shard_map/all_to_all | solution.py:90
  49.6 13.1 %all-gather.10.cloned.1.call-done = bf16[1,2048,1024]{2,1,0:T(8,128)(2,1)} async-done(((bf16[1,256,1024]{2,1,0:T(8,128)(2,1)}), bf16[1,2048,1024]{2,1,0:T(8,128)(2,1)}) %all-gather.10.cloned.1.call-update) | async-done | bytes 4194320 | tf_op jit(solution)/shard_map/all_gather | solution.py:70
  62.7 3.7 %fusion.12 = f32[128,1024]{1,0:T(8,128)} fusion(bf16[128,2048]{1,0:T(8,128)(2,1)S(1)} %bitcast.90, bf16[1,2048,1024]{2,1,0:T(8,128)(2,1)} %all-gather.10.cloned.1.call-done), kind=kOutput, calls=%fused_computation.12 | convolution fusion | flops 536870912 | bytes 5242880 | tf_op jit(solution)/shard_map/dot_general | solution.py:51
  66.4 44.0 %all-gather.14.cloned.1.call-done = bf16[1,2048,1024]{2,1,0:T(8,128)(2,1)} async-done(((bf16[1,256,1024]{2,1,0:T(8,128)(2,1)}), bf16[1,2048,1024]{2,1,0:T(8,128)(2,1)}) %all-gather.14.cloned.1.call-update) | async-done | bytes 4194320 | tf_op jit(solution)/shard_map/all_gather | solution.py:72
  110.3 3.7 %fusion.2 = f32[128,1024]{1,0:T(8,128)} fusion(bf16[128,2048]{1,0:T(8,128)(2,1)S(1)} %bitcast.93, bf16[1,2048,1024]{2,1,0:T(8,128)(2,1)} %all-gather.14.cloned.1.call-done), kind=kOutput, calls=%fused_computation.2 | convolution fusion | flops 536870912 | bytes 5242880 | tf_op jit(solution)/shard_map/dot_general | solution.py:55
  114.0 43.8 %all-gather.12.cloned.1.call-done = bf16[1,2048,1024]{2,1,0:T(8,128)(2,1)} async-done(((bf16[1,256,1024]{2,1,0:T(8,128)(2,1)}), bf16[1,2048,1024]{2,1,0:T(8,128)(2,1)}) %all-gather.12.cloned.1.call-update) | async-done | bytes 4194320 | tf_op jit(solution)/shard_map/all_gather | solution.py:71
  157.8 3.4 %multiply_convert_fusion.2 = (bf16[128,1024]{1,0:T(8,128)(2,1)S(1)}, bf16[128,1024]{1,0:T(8,128)(2,1)S(1)}, bf16[128,1024]{1,0:T(8,128)(2,1)S(1)}) fusion(f32[128,1024]{1,0:T(8,128)} %fusion.12, f32[128,1024]{1,0:T(8,128)} %fusion.2, bf16[128,2048]{1,0:T(8,128)(2,1)S(1)} %bitcast.91, bf16[1,2048,1024]{2,1,0:T(8,128)(2,1)} %all-gather.12.cloned.1.call-done), kind=kOutput, calls=%fused_computation.56 | convolution fusion | flops 538968064 | bytes 6553600 | tf_op jit(solution)/shard_map/dot_general | solution.py:52
  163.8 3.6 %all-to-all-start.6 = ((bf16[8,2,128,256]{3,2,1,0:T(8,128)(2,1)}), bf16[8,2,128,256]{3,2,1,0:T(8,128)(2,1)S(1)}, u32[]{:S(2)}, u32[]{:S(2)}) async-start(bf16[8,2,128,256]{3,2,1,0:T(8,128)(2,1)} %copy.121), calls=%async_computation.6 | async-start | bytes 2097152 | tf_op jit(solution)/shard_map/all_to_all | solution.py:94
  167.3 4.2 %fusion.24 = bf16[128,2048]{1,0:T(8,128)(2,1)S(1)} fusion(bf16[128,1024]{1,0:T(8,128)(2,1)S(1)} %get-tuple-element.17, bf16[1,2048,1024]{2,1,0:T(8,128)(2,1)} %all-gather.14.cloned.1.call-done), kind=kOutput, calls=%fused_computation.21 | convolution fusion | flops 537133056 | bytes 4980736 | tf_op jit(solution)/shard_map/dot_general | solution.py:103
  171.5 3.7 %fusion.6 = f32[128,2048]{1,0:T(8,128)S(1)} fusion(bf16[128,1024]{1,0:T(8,128)(2,1)S(1)} %get-tuple-element.19, bf16[1,2048,1024]{2,1,0:T(8,128)(2,1)} %all-gather.12.cloned.1.call-done), kind=kOutput, calls=%fused_computation.6 | convolution fusion | flops 536870912 | bytes 5505024 | tf_op jit(solution)/shard_map/dot_general | solution.py:106
  177.8 43.4 %all-to-all-done.6 = bf16[8,2,128,256]{3,2,1,0:T(8,128)(2,1)S(1)} async-done(((bf16[8,2,128,256]{3,2,1,0:T(8,128)(2,1)}), bf16[8,2,128,256]{3,2,1,0:T(8,128)(2,1)S(1)}, u32[]{:S(2)}, u32[]{:S(2)}) %all-to-all-start.6) | async-done | bytes 1048608 | tf_op jit(solution)/shard_map/all_to_all | solution.py:94
  221.3 3.6 %all-to-all-start.2 = ((bf16[4,2,32,2048]{3,2,1,0:T(8,128)(2,1)}), bf16[4,2,32,2048]{3,2,1,0:T(8,128)(2,1)S(1)}, u32[]{:S(2)}, u32[]{:S(2)}) async-start(bf16[4,2,32,2048]{3,2,1,0:T(8,128)(2,1)} %pad_maximum_fusion.1), calls=%async_computation.2 | async-start | bytes 2097152 | tf_op jit(solution)/shard_map/all_to_all | solution.py:111
  227.1 8.4 %all-to-all-done.2 = bf16[4,2,32,2048]{3,2,1,0:T(8,128)(2,1)S(1)} async-done(((bf16[4,2,32,2048]{3,2,1,0:T(8,128)(2,1)}), bf16[4,2,32,2048]{3,2,1,0:T(8,128)(2,1)S(1)}, u32[]{:S(2)}, u32[]{:S(2)}) %all-to-all-start.2) | async-done | bytes 1048608 | tf_op jit(solution)/shard_map/all_to_all | solution.py:111
  240.6 6.6 %all-to-all-start.4 = ((bf16[8,256,64]{1,2,0:T(8,128)(2,1)}), bf16[8,256,64]{1,2,0:T(8,128)(2,1)S(1)}, u32[]{:S(2)}, u32[]{:S(2)}) async-start(bf16[8,256,64]{1,2,0:T(8,128)(2,1)} %bitcast.89), calls=%async_computation.4 | async-start | bytes 524288 | tf_op jit(solution)/shard_map/all_to_all | solution.py:121
  249.8 7.1 %all-to-all-done.4 = bf16[8,256,64]{1,2,0:T(8,128)(2,1)S(1)} async-done(((bf16[8,256,64]{1,2,0:T(8,128)(2,1)}), bf16[8,256,64]{1,2,0:T(8,128)(2,1)S(1)}, u32[]{:S(2)}, u32[]{:S(2)}) %all-to-all-start.4) | async-done | bytes 262176 | tf_op jit(solution)/shard_map/all_to_all | solution.py:121
  257.7 2.8 all-to-all-start.3
  260.5 1.7 fusion.43
  262.2 9.2 %all-to-all-done.3 = f32[32,1,2048]{2,1,0:T(1,128)S(1)} async-done(((f32[32,1,2048]{2,1,0:T(1,128)}), f32[32,1,2048]{2,1,0:T(1,128)S(1)}, u32[]{:S(2)}, u32[]{:S(2)}) %all-to-all-start.3) | async-done | bytes 262176 | tf_op jit(solution)/shard_map/all_to_all | solution.py:47
  272.1 3.4 %all-to-all-start.5 = ((f32[4,256,64]{1,2,0:T(8,128)}), f32[4,256,64]{1,2,0:T(8,128)S(1)}, u32[]{:S(2)}, u32[]{:S(2)}) async-start(f32[4,256,64]{1,2,0:T(8,128)} %broadcast_in_dim.31), calls=%async_computation.5 | async-start | bytes 524288 | tf_op jit(solution)/shard_map/all_to_all | solution.py:47
  277.7 3.2 %all-to-all-done.5 = f32[4,256,64]{1,2,0:T(8,128)S(1)} async-done(((f32[4,256,64]{1,2,0:T(8,128)}), f32[4,256,64]{1,2,0:T(8,128)S(1)}, u32[]{:S(2)}, u32[]{:S(2)}) %all-to-all-start.5) | async-done | bytes 262176 | tf_op jit(solution)/shard_map/all_to_all | solution.py:47
  281.6 3.7 %fusion.15 = bf16[256,2048]{1,0:T(8,128)(2,1)S(1)} fusion(bf16[1024,256]{1,0:T(8,128)(2,1)} %bitcast.108, bf16[1024,3072]{1,0:T(8,128)(2,1)} %all-gather.8.cloned.1.call-done), kind=kOutput, calls=%fused_computation.16 | convolution fusion | flops 1074266112 | bytes 5767168 | tf_op jit(solution)/shard_map/dot_general | solution.py:137
  286.3 3.1 %fusion.35 = bf16[1,256,1024]{2,1,0:T(8,128)(2,1)} fusion(bf16[1024,256]{1,0:T(8,128)(2,1)S(1)} %bitcast.103, bf16[1024,3072]{1,0:T(8,128)(2,1)} %all-gather.8.cloned.1.call-done), kind=kOutput, calls=%fused_computation.37 | convolution fusion | flops 537133056 | bytes 3145728 | tf_op jit(solution)/shard_map/dot_general | solution.py:143
  (81 shorter events, 29.2 us)
Async XLA Ops:
  7.2 26.1 %copy-start = (bf16[128,2048]{1,0:T(8,128)(2,1)S(1)}, bf16[128,2048]{1,0:T(8,128)(2,1)}, u32[]{:S(2)}) copy-start(bf16[128,2048]{1,0:T(8,128)(2,1)} %param.15) | copy-start | bytes 1572868
  7.2 24.6 %copy-start.6 = (s32[128,8]{0,1:T(8,128)S(1)}, s32[128,8]{0,1:T(8,128)}, u32[]{:S(2)}) copy-start(s32[128,8]{0,1:T(8,128)} %param.11) | copy-start | bytes 12292
  7.2 12.4 %copy-start.2 = (bf16[128,2048]{1,0:T(8,128)(2,1)S(1)}, bf16[128,2048]{1,0:T(8,128)(2,1)}, u32[]{:S(2)}) copy-start(bf16[128,2048]{1,0:T(8,128)(2,1)} %param.8) | copy-start | bytes 1572868
  7.2 24.2 %copy-start.5 = (f32[2048]{0:T(1024)S(1)}, f32[2048]{0:T(1024)}, u32[]{:S(2)}) copy-start(f32[2048]{0:T(1024)} %param.9) | copy-start | bytes 24580
  7.2 55.5 %all-gather.10.cloned.1.call-start = ((), (), s32[]{:S(2)}) async-start(), calls=%async_computation.8 | async-start | bytes 4718592 | tf_op jit(solution)/shard_map/all_gather | solution.py:70
  7.9 102.4 %all-gather.14.cloned.1.call-start = ((), (), s32[]{:S(2)}) async-start(), calls=%async_computation.10 | async-start | bytes 4718592 | tf_op jit(solution)/shard_map/all_gather | solution.py:72
  8.7 149.1 %all-gather.12.cloned.1.call-start = ((), (), s32[]{:S(2)}) async-start(), calls=%async_computation.9 | async-start | bytes 4718592 | tf_op jit(solution)/shard_map/all_gather | solution.py:71
  10.9 20.4 %all-to-all-start = ((bf16[8,256,64]{1,2,0:T(8,128)(2,1)}), bf16[8,256,64]{1,2,0:T(8,128)(2,1)S(1)}, u32[]{:S(2)}, u32[]{:S(2)}) async-start(bf16[8,256,64]{1,2,0:T(8,128)(2,1)} %broadcast_in_dim.25), calls=%async_computation | async-start | bytes 524288 | tf_op jit(solution)/shard_map/all_to_all | solution.py:47
  17.2 264.3 %all-gather.8.cloned.1.call-start = ((), (), s32[]{:S(2)}) async-start(), calls=%async_computation.7 | async-start | bytes 7077888 | tf_op jit(solution)/shard_map/all_gather | solution.py:100
  19.8 11.6 %copy-start.9 = (f32[128]{0:T(128)}, f32[128]{0:T(128)S(1)}, u32[]{:S(2)}) copy-start(f32[128]{0:T(128)S(1)} %fusion.44) | copy-start | bytes 1540
  19.8 14.2 %copy-start.8 = (f32[128]{0:T(128)}, f32[128]{0:T(128)S(1)}, u32[]{:S(2)}) copy-start(f32[128]{0:T(128)S(1)} %fusion.47) | copy-start | bytes 1540
  31.8 0.5 copy-start.7
  32.8 1.1 copy-start.4
  163.8 57.5 %all-to-all-start.6 = ((bf16[8,2,128,256]{3,2,1,0:T(8,128)(2,1)}), bf16[8,2,128,256]{3,2,1,0:T(8,128)(2,1)S(1)}, u32[]{:S(2)}, u32[]{:S(2)}) async-start(bf16[8,2,128,256]{3,2,1,0:T(8,128)(2,1)} %copy.121), calls=%async_computation.6 | async-start | bytes 2097152 | tf_op jit(solution)/shard_map/all_to_all | solution.py:94
  167.3 7.9 %copy-start.1 = (bf16[1,2048,1024]{2,1,0:T(8,128)(2,1)S(1)}, bf16[1,2048,1024]{2,1,0:T(8,128)(2,1)}, u32[]{:S(2)}) copy-start(bf16[1,2048,1024]{2,1,0:T(8,128)(2,1)} %all-gather.10.cloned.1.call-done) | copy-start | bytes 12582916
  221.3 14.3 %all-to-all-start.2 = ((bf16[4,2,32,2048]{3,2,1,0:T(8,128)(2,1)}), bf16[4,2,32,2048]{3,2,1,0:T(8,128)(2,1)S(1)}, u32[]{:S(2)}, u32[]{:S(2)}) async-start(bf16[4,2,32,2048]{3,2,1,0:T(8,128)(2,1)} %pad_maximum_fusion.1), calls=%async_computation.2 | async-start | bytes 2097152 | tf_op jit(solution)/shard_map/all_to_all | solution.py:111
  235.7 14.1 %copy-start.10 = (f32[128]{0:T(128)S(1)}, f32[128]{0:T(128)}, u32[]{:S(2)}) copy-start(f32[128]{0:T(128)} %copy-done.9) | copy-start | bytes 1540
  240.6 16.3 %all-to-all-start.4 = ((bf16[8,256,64]{1,2,0:T(8,128)(2,1)}), bf16[8,256,64]{1,2,0:T(8,128)(2,1)S(1)}, u32[]{:S(2)}, u32[]{:S(2)}) async-start(bf16[8,256,64]{1,2,0:T(8,128)(2,1)} %bitcast.89), calls=%async_computation.4 | async-start | bytes 524288 | tf_op jit(solution)/shard_map/all_to_all | solution.py:121
  257.7 13.7 %all-to-all-start.3 = ((f32[32,1,2048]{2,1,0:T(1,128)}), f32[32,1,2048]{2,1,0:T(1,128)S(1)}, u32[]{:S(2)}, u32[]{:S(2)}) async-start(f32[32,1,2048]{2,1,0:T(1,128)} %broadcast_in_dim.30), calls=%async_computation.3 | async-start | bytes 524288 | tf_op jit(solution)/shard_map/all_to_all | solution.py:47
  272.1 8.8 %all-to-all-start.5 = ((f32[4,256,64]{1,2,0:T(8,128)}), f32[4,256,64]{1,2,0:T(8,128)S(1)}, u32[]{:S(2)}, u32[]{:S(2)}) async-start(f32[4,256,64]{1,2,0:T(8,128)} %broadcast_in_dim.31), calls=%async_computation.5 | async-start | bytes 524288 | tf_op jit(solution)/shard_map/all_to_all | solution.py:47
  281.5 4.7 %copy-start.3 = (bf16[8,1,128,256]{3,2,1,0:T(8,128)(2,1)S(1)}, bf16[8,1,128,256]{3,2,1,0:T(8,128)(2,1)}, u32[]{:S(2)}) copy-start(bf16[8,1,128,256]{3,2,1,0:T(8,128)(2,1)} %get-tuple-element.11) | copy-start | bytes 1572868
Sparse Core Ops, SparseCore 0:
  9.6 52.9 all-gather.9
  64.3 46.0 all-gather.13
  111.9 45.8 all-gather.11
  162.3 83.6 all-gather.7

commit v3 on v2

--- a/solution.py
+++ b/solution.py
@@ -94,9 +94,10 @@
     cut = lax.all_to_all(
         cut.transpose(2, 0, 1, 3), "dp", split_axis=0, concat_axis=0, tiled=True
     )
+    cut, late_grads = lax.optimization_barrier((cut, flat_grads))
     rows_cut = cut[:, 0].reshape(groups_dp * slot_count, shard_rows)
     grads_cut = cut[:, 1].reshape(groups_dp * slot_count, shard_rows)
-    active, grad_gate, grad_upper = expert_pass(flat_rows, flat_grads, w_gate, w_up, w_down)
+    active, grad_gate, grad_upper = expert_pass(flat_rows, late_grads, w_gate, w_up, w_down)
     units = lax.all_gather(
         jnp.concatenate([grad_gate, grad_upper, active], axis=1), "dp", axis=0, tiled=True
     )

time: 297 us -> 272 us (0.916)
  waiting for transfers between devices: 186 us -> 130 us
  blocking collectives: 15.5 us -> 51 us
  starting transfers between devices: 26.4 us -> 21.6 us
    all_to_all x1 -> x0, waiting for transfers between devices: 43.4 us -> none  [body(): lax.all_to_all(cut.transpose(2, 0, 1, 3), 'dp', split_axis=0, concat_axis...]
    all_to_all x0 -> x1, blocking collectives: none -> 35.5 us  [body(): lax.all_to_all(cut.transpose(2, 0, 1, 3), 'dp', split_axis=0, concat_axis...]
    all_gather x1, waiting for transfers between devices: 44 us -> 29.8 us  [body(): w_down = lax.all_gather(down_weight[0], 'dp', axis=0, tiled=True)]
    all_gather x1, waiting for transfers between devices: 13.1 us -> 0.01 us  [body(): w_gate = lax.all_gather(gate_weight[0], 'dp', axis=0, tiled=True)]
    all_to_all x1, waiting for transfers between devices: 7.07 us -> 13.5 us  [body(): lax.all_to_all(grad_router.astype(jnp.bfloat16).reshape(groups_dp, shard_...]
    all_to_all x3, waiting for transfers between devices: 23.9 us -> 28.3 us  [small_gather(): return lax.all_to_all(copies, axis, split_axis=0, concat_axis=0, tiled=True)]
    all_to_all x1, waiting for transfers between devices: 8.45 us -> 12.8 us  [body(): lax.all_to_all(produced, 'expert', split_axis=0, concat_axis=0, tiled=True)]
    all_to_all x1 -> x0, starting transfers between devices: 3.56 us -> none  [body(): lax.all_to_all(cut.transpose(2, 0, 1, 3), 'dp', split_axis=0, concat_axis...]
  transfers between devices with their start and end apart: 10 -> 9, of which waited for: 9 -> 7; matrix products, arithmetic and copies ran while one was open for 14% -> 15% of each run, Pallas kernels for 0% -> 0%
where the time goes in v3:
time: 272 us; the launch traced here: 271 us
  waiting for transfers between devices  130 us (48%)
  blocking collectives  51 us (19%)
  matrix products  34.4 us (13%)
  starting transfers between devices  21.6 us (8%)
  between operations  14.2 us (5%)
  local copies, waits for them, and re-layouts  10.2 us (4%)
  other arithmetic  9.06 us (3%)
    all_gather x1, waiting for transfers between devices, body(): w_up = lax.all_gather(up_weight[0], 'dp', axis=0, tiled=True)  43.9 us
    all_to_all x1, blocking collectives, body(): lax.all_to_all(cut.transpose(2, 0, 1, 3), 'dp', split_axis=0, concat_axis...  35.5 us
    all_gather x1, waiting for transfers between devices, body(): w_down = lax.all_gather(down_weight[0], 'dp', axis=0, tiled=True)  29.8 us
    all_to_all x3, waiting for transfers between devices, small_gather(): return lax.all_to_all(copies, axis, split_axis=0, concat_axis=0, tiled=True)  28.3 us
    all_to_all x1, blocking collectives, body(): lax.all_to_all(leaving, 'expert', split_axis=0, concat_axis=0, tiled=True)  15.5 us
    all_to_all x3, starting transfers between devices, small_gather(): return lax.all_to_all(copies, axis, split_axis=0, concat_axis=0, tiled=True)  13.8 us
    all_to_all x1, waiting for transfers between devices, body(): lax.all_to_all(grad_router.astype(jnp.bfloat16).reshape(groups_dp, shard_...  13.5 us
    all_to_all x1, waiting for transfers between devices, body(): lax.all_to_all(produced, 'expert', split_axis=0, concat_axis=0, tiled=True)  12.8 us
  transfers between devices with their start and end apart: 9, of which 7 were waited for; matrix products, arithmetic and copies ran while one was open for 15% of the time, Pallas kernels for 0%

profile of v3, /device:TPU:0, one launch (start us, length us, event | category | flops | bytes accessed | tf_op | source)
XLA Modules:
  0.0 270.7 jit_solution(8275553459467898852)
XLA Ops:
  9.4 1.5 broadcast_in_dim.25
  10.9 6.3 %all-to-all-start = ((bf16[8,256,64]{1,2,0:T(8,128)(2,1)}), bf16[8,256,64]{1,2,0:T(8,128)(2,1)S(1)}, u32[]{:S(2)}, u32[]{:S(2)}) async-start(bf16[8,256,64]{1,2,0:T(8,128)(2,1)} %broadcast_in_dim.25), calls=%async_computation | async-start | bytes 524288 | tf_op jit(solution)/shard_map/all_to_all | solution.py:47
  19.8 11.5 %all-to-all-done = bf16[8,256,64]{1,2,0:T(8,128)(2,1)S(1)} async-done(((bf16[8,256,64]{1,2,0:T(8,128)(2,1)}), bf16[8,256,64]{1,2,0:T(8,128)(2,1)S(1)}, u32[]{:S(2)}, u32[]{:S(2)}) %all-to-all-start) | async-done | bytes 262176 | tf_op jit(solution)/shard_map/all_to_all | solution.py:47
  34.0 15.5 %all_to_all.36 = bf16[4,2,32,2048]{3,2,1,0:T(8,128)(2,1)S(1)} all-to-all(bf16[4,2,32,2048]{3,2,1,0:T(8,128)(2,1)S(1)} %pad_maximum_fusion), channel_id=1, replica_groups=mesh['dp'=8,'expert'=4] {'expert'}, dimensions={0} | all-to-all | bytes 2097152 | tf_op jit(solution)/shard_map/all_to_all | solution.py:90
  50.2 35.5 %all_to_all.37 = bf16[8,2,128,256]{3,2,1,0:T(8,128)(2,1)S(1)} all-to-all(bf16[8,2,128,256]{3,2,1,0:T(8,128)(2,1)S(1)} %copy.114), channel_id=1, replica_groups=mesh['dp'=8,'expert'=4] {'dp'}, dimensions={0} | all-to-all | bytes 2097152 | tf_op jit(solution)/shard_map/all_to_all | solution.py:94
  85.7 3.7 %fusion.12 = f32[128,1024]{1,0:T(8,128)} fusion(bf16[128,2048]{1,0:T(8,128)(2,1)S(1)} %bitcast.87, bf16[1,2048,1024]{2,1,0:T(8,128)(2,1)} %all-gather.10.cloned.1.call-done), kind=kOutput, calls=%fused_computation.12 | convolution fusion | flops 536870912 | bytes 5242880 | tf_op jit(solution)/shard_map/dot_general | solution.py:51
  89.4 29.8 %all-gather.14.cloned.1.call-done = bf16[1,2048,1024]{2,1,0:T(8,128)(2,1)} async-done(((bf16[1,256,1024]{2,1,0:T(8,128)(2,1)}), bf16[1,2048,1024]{2,1,0:T(8,128)(2,1)}) %all-gather.14.cloned.1.call-update) | async-done | bytes 4194320 | tf_op jit(solution)/shard_map/all_gather | solution.py:72
  119.2 3.7 %fusion.2 = f32[128,1024]{1,0:T(8,128)} fusion(bf16[128,2048]{1,0:T(8,128)(2,1)S(1)} %bitcast.90, bf16[1,2048,1024]{2,1,0:T(8,128)(2,1)} %all-gather.14.cloned.1.call-done), kind=kOutput, calls=%fused_computation.2 | convolution fusion | flops 536870912 | bytes 5242880 | tf_op jit(solution)/shard_map/dot_general | solution.py:55
  122.9 43.9 %all-gather.12.cloned.1.call-done = bf16[1,2048,1024]{2,1,0:T(8,128)(2,1)} async-done(((bf16[1,256,1024]{2,1,0:T(8,128)(2,1)}), bf16[1,2048,1024]{2,1,0:T(8,128)(2,1)}) %all-gather.12.cloned.1.call-update) | async-done | bytes 4194320 | tf_op jit(solution)/shard_map/all_gather | solution.py:71
  166.8 3.4 %multiply_convert_fusion.2 = (bf16[128,1024]{1,0:T(8,128)(2,1)S(1)}, bf16[128,1024]{1,0:T(8,128)(2,1)S(1)}, bf16[128,1024]{1,0:T(8,128)(2,1)S(1)}) fusion(f32[128,1024]{1,0:T(8,128)} %fusion.12, f32[128,1024]{1,0:T(8,128)} %fusion.2, bf16[128,2048]{1,0:T(8,128)(2,1)S(1)} %bitcast.88, bf16[1,2048,1024]{2,1,0:T(8,128)(2,1)} %all-gather.12.cloned.1.call-done), kind=kOutput, calls=%fused_computation.56 | convolution fusion | flops 538968064 | bytes 6553600 | tf_op jit(solution)/shard_map/dot_general | solution.py:52
  171.9 3.8 %fusion.24 = bf16[128,2048]{1,0:T(8,128)(2,1)S(1)} fusion(bf16[128,1024]{1,0:T(8,128)(2,1)S(1)} %get-tuple-element.21, bf16[1,2048,1024]{2,1,0:T(8,128)(2,1)} %all-gather.14.cloned.1.call-done), kind=kOutput, calls=%fused_computation.21 | convolution fusion | flops 537133056 | bytes 4980736 | tf_op jit(solution)/shard_map/dot_general | solution.py:104
  175.7 3.9 %fusion.6 = f32[128,2048]{1,0:T(8,128)S(1)} fusion(bf16[128,1024]{1,0:T(8,128)(2,1)S(1)} %copy-done.5, bf16[1,2048,1024]{2,1,0:T(8,128)(2,1)} %all-gather.12.cloned.1.call-done), kind=kOutput, calls=%fused_computation.6 | convolution fusion | flops 536870912 | bytes 5505024 | tf_op jit(solution)/shard_map/dot_general | solution.py:107
  179.7 1.5 fusion.21
  182.3 4.2 %all-to-all-start.3 = ((bf16[4,2,32,2048]{3,2,1,0:T(8,128)(2,1)}), bf16[4,2,32,2048]{3,2,1,0:T(8,128)(2,1)}, u32[]{:S(2)}, u32[]{:S(2)}) async-start(bf16[4,2,32,2048]{3,2,1,0:T(8,128)(2,1)} %pad_maximum_fusion.1), calls=%async_computation.3 | async-start | bytes 2097152 | tf_op jit(solution)/shard_map/all_to_all | solution.py:112
  188.1 12.8 %all-to-all-done.3 = bf16[4,2,32,2048]{3,2,1,0:T(8,128)(2,1)} async-done(((bf16[4,2,32,2048]{3,2,1,0:T(8,128)(2,1)}), bf16[4,2,32,2048]{3,2,1,0:T(8,128)(2,1)}, u32[]{:S(2)}, u32[]{:S(2)}) %all-to-all-start.3) | async-done | bytes 1048608 | tf_op jit(solution)/shard_map/all_to_all | solution.py:112
  207.1 3.4 %all-to-all-start.5 = ((bf16[8,256,64]{1,2,0:T(8,128)(2,1)}), bf16[8,256,64]{1,2,0:T(8,128)(2,1)S(1)}, u32[]{:S(2)}, u32[]{:S(2)}) async-start(bf16[8,256,64]{1,2,0:T(8,128)(2,1)} %bitcast.85), calls=%async_computation.5 | async-start | bytes 524288 | tf_op jit(solution)/shard_map/all_to_all | solution.py:122
  212.5 13.5 %all-to-all-done.5 = bf16[8,256,64]{1,2,0:T(8,128)(2,1)S(1)} async-done(((bf16[8,256,64]{1,2,0:T(8,128)(2,1)}), bf16[8,256,64]{1,2,0:T(8,128)(2,1)S(1)}, u32[]{:S(2)}, u32[]{:S(2)}) %all-to-all-start.5) | async-done | bytes 262176 | tf_op jit(solution)/shard_map/all_to_all | solution.py:122
  226.9 4.0 %all-to-all-start.4 = ((f32[32,1,2048]{2,1,0:T(1,128)}), f32[32,1,2048]{2,1,0:T(1,128)S(1)}, u32[]{:S(2)}, u32[]{:S(2)}) async-start(f32[32,1,2048]{2,1,0:T(1,128)} %broadcast_in_dim.30), calls=%async_computation.4 | async-start | bytes 524288 | tf_op jit(solution)/shard_map/all_to_all | solution.py:47
  230.9 1.7 fusion.43
  232.7 13.0 %all-to-all-done.4 = f32[32,1,2048]{2,1,0:T(1,128)S(1)} async-done(((f32[32,1,2048]{2,1,0:T(1,128)}), f32[32,1,2048]{2,1,0:T(1,128)S(1)}, u32[]{:S(2)}, u32[]{:S(2)}) %all-to-all-start.4) | async-done | bytes 262176 | tf_op jit(solution)/shard_map/all_to_all | solution.py:47
  246.4 3.4 %all-to-all-start.6 = ((f32[4,256,64]{1,2,0:T(8,128)}), f32[4,256,64]{1,2,0:T(8,128)S(1)}, u32[]{:S(2)}, u32[]{:S(2)}) async-start(f32[4,256,64]{1,2,0:T(8,128)} %broadcast_in_dim.31), calls=%async_computation.6 | async-start | bytes 524288 | tf_op jit(solution)/shard_map/all_to_all | solution.py:47
  251.9 3.8 %all-to-all-done.6 = f32[4,256,64]{1,2,0:T(8,128)S(1)} async-done(((f32[4,256,64]{1,2,0:T(8,128)}), f32[4,256,64]{1,2,0:T(8,128)S(1)}, u32[]{:S(2)}, u32[]{:S(2)}) %all-to-all-start.6) | async-done | bytes 262176 | tf_op jit(solution)/shard_map/all_to_all | solution.py:47
  256.4 3.7 %fusion.15 = bf16[256,2048]{1,0:T(8,128)(2,1)S(1)} fusion(bf16[1024,256]{1,0:T(8,128)(2,1)} %bitcast.104, bf16[1024,3072]{1,0:T(8,128)(2,1)} %all-gather.8.cloned.1.call-done), kind=kOutput, calls=%fused_computation.16 | convolution fusion | flops 1074266112 | bytes 5767168 | tf_op jit(solution)/shard_map/dot_general | solution.py:138
  261.1 3.1 %fusion.35 = bf16[1,256,1024]{2,1,0:T(8,128)(2,1)} fusion(bf16[1024,256]{1,0:T(8,128)(2,1)S(1)} %bitcast.99, bf16[1024,3072]{1,0:T(8,128)(2,1)} %all-gather.8.cloned.1.call-done), kind=kOutput, calls=%fused_computation.37 | convolution fusion | flops 537133056 | bytes 3145728 | tf_op jit(solution)/shard_map/dot_general | solution.py:144
  (88 shorter events, 25.8 us)
Async XLA Ops:
  7.2 26.1 %copy-start = (bf16[128,2048]{1,0:T(8,128)(2,1)S(1)}, bf16[128,2048]{1,0:T(8,128)(2,1)}, u32[]{:S(2)}) copy-start(bf16[128,2048]{1,0:T(8,128)(2,1)} %param.15) | copy-start | bytes 1572868
  7.2 24.6 %copy-start.8 = (s32[128,8]{0,1:T(8,128)S(1)}, s32[128,8]{0,1:T(8,128)}, u32[]{:S(2)}) copy-start(s32[128,8]{0,1:T(8,128)} %param.11) | copy-start | bytes 12292
  7.2 12.4 %copy-start.2 = (bf16[128,2048]{1,0:T(8,128)(2,1)S(1)}, bf16[128,2048]{1,0:T(8,128)(2,1)}, u32[]{:S(2)}) copy-start(bf16[128,2048]{1,0:T(8,128)(2,1)} %param.8) | copy-start | bytes 1572868
  7.2 24.2 %copy-start.7 = (f32[2048]{0:T(1024)S(1)}, f32[2048]{0:T(1024)}, u32[]{:S(2)}) copy-start(f32[2048]{0:T(1024)} %param.9) | copy-start | bytes 24580
  7.2 78.4 %all-gather.10.cloned.1.call-start = ((), (), s32[]{:S(2)}) async-start(), calls=%async_computation.8 | async-start | bytes 4718592 | tf_op jit(solution)/shard_map/all_gather | solution.py:70
  7.9 111.2 %all-gather.14.cloned.1.call-start = ((), (), s32[]{:S(2)}) async-start(), calls=%async_computation.10 | async-start | bytes 4718592 | tf_op jit(solution)/shard_map/all_gather | solution.py:72
  8.7 158.1 %all-gather.12.cloned.1.call-start = ((), (), s32[]{:S(2)}) async-start(), calls=%async_computation.9 | async-start | bytes 4718592 | tf_op jit(solution)/shard_map/all_gather | solution.py:71
  10.9 20.4 %all-to-all-start = ((bf16[8,256,64]{1,2,0:T(8,128)(2,1)}), bf16[8,256,64]{1,2,0:T(8,128)(2,1)S(1)}, u32[]{:S(2)}, u32[]{:S(2)}) async-start(bf16[8,256,64]{1,2,0:T(8,128)(2,1)} %broadcast_in_dim.25), calls=%async_computation | async-start | bytes 524288 | tf_op jit(solution)/shard_map/all_to_all | solution.py:47
  17.2 239.1 %all-gather.8.cloned.1.call-start = ((), (), s32[]{:S(2)}) async-start(), calls=%async_computation.7 | async-start | bytes 7077888 | tf_op jit(solution)/shard_map/all_gather | solution.py:101
  19.8 11.6 %copy-start.13 = (f32[128]{0:T(128)}, f32[128]{0:T(128)S(1)}, u32[]{:S(2)}) copy-start(f32[128]{0:T(128)S(1)} %fusion.44) | copy-start | bytes 1540
  19.8 14.2 %copy-start.11 = (f32[128]{0:T(128)}, f32[128]{0:T(128)S(1)}, u32[]{:S(2)}) copy-start(f32[128]{0:T(128)S(1)} %fusion.47) | copy-start | bytes 1540
  31.8 0.5 copy-start.9
  32.8 1.1 copy-start.6
  170.2 0.7 copy-start.4
  171.8 3.9 %copy-start.5 = (bf16[128,1024]{1,0:T(8,128)(2,1)S(1)}, bf16[128,1024]{1,0:T(8,128)(2,1)}, u32[]{:S(2)}) copy-start(bf16[128,1024]{1,0:T(8,128)(2,1)} %copy-done.4) | copy-start | bytes 786436
  171.9 7.8 %copy-start.1 = (bf16[1,2048,1024]{2,1,0:T(8,128)(2,1)S(1)}, bf16[1,2048,1024]{2,1,0:T(8,128)(2,1)}, u32[]{:S(2)}) copy-start(bf16[1,2048,1024]{2,1,0:T(8,128)(2,1)} %all-gather.10.cloned.1.call-done) | copy-start | bytes 12582916
  179.7 6.9 %copy-start.10 = (f32[128]{0:T(128)S(1)}, f32[128]{0:T(128)}, u32[]{:S(2)}) copy-start(f32[128]{0:T(128)} %copy-done.9) | copy-start | bytes 1540
  182.3 18.6 %all-to-all-start.3 = ((bf16[4,2,32,2048]{3,2,1,0:T(8,128)(2,1)}), bf16[4,2,32,2048]{3,2,1,0:T(8,128)(2,1)}, u32[]{:S(2)}, u32[]{:S(2)}) async-start(bf16[4,2,32,2048]{3,2,1,0:T(8,128)(2,1)} %pad_maximum_fusion.1), calls=%async_computation.3 | async-start | bytes 2097152 | tf_op jit(solution)/shard_map/all_to_all | solution.py:112
  188.1 23.4 %copy-start.12 = (f32[128]{0:T(128)S(1)}, f32[128]{0:T(128)}, u32[]{:S(2)}) copy-start(f32[128]{0:T(128)} %copy-done.11) | copy-start | bytes 1540
  202.2 10.3 %copy-start.14 = (f32[128]{0:T(128)S(1)}, f32[128]{0:T(128)}, u32[]{:S(2)}) copy-start(f32[128]{0:T(128)} %copy-done.13) | copy-start | bytes 1540
  207.1 19.0 %all-to-all-start.5 = ((bf16[8,256,64]{1,2,0:T(8,128)(2,1)}), bf16[8,256,64]{1,2,0:T(8,128)(2,1)S(1)}, u32[]{:S(2)}, u32[]{:S(2)}) async-start(bf16[8,256,64]{1,2,0:T(8,128)(2,1)} %bitcast.85), calls=%async_computation.5 | async-start | bytes 524288 | tf_op jit(solution)/shard_map/all_to_all | solution.py:122
  226.9 18.8 %all-to-all-start.4 = ((f32[32,1,2048]{2,1,0:T(1,128)}), f32[32,1,2048]{2,1,0:T(1,128)S(1)}, u32[]{:S(2)}, u32[]{:S(2)}) async-start(f32[32,1,2048]{2,1,0:T(1,128)} %broadcast_in_dim.30), calls=%async_computation.4 | async-start | bytes 524288 | tf_op jit(solution)/shard_map/all_to_all | solution.py:47
  246.4 9.4 %all-to-all-start.6 = ((f32[4,256,64]{1,2,0:T(8,128)}), f32[4,256,64]{1,2,0:T(8,128)S(1)}, u32[]{:S(2)}, u32[]{:S(2)}) async-start(f32[4,256,64]{1,2,0:T(8,128)} %broadcast_in_dim.31), calls=%async_computation.6 | async-start | bytes 524288 | tf_op jit(solution)/shard_map/all_to_all | solution.py:47
  256.4 4.7 %copy-start.3 = (bf16[8,1,128,256]{3,2,0,1:T(8,128)(2,1)S(1)}, bf16[8,1,128,256]{3,2,0,1:T(8,128)(2,1)}, u32[]{:S(2)}) copy-start(bf16[8,1,128,256]{3,2,0,1:T(8,128)(2,1)} %get-tuple-element.15) | copy-start | bytes 1572868
Sparse Core Ops, SparseCore 0:
  9.6 53.2 all-gather.9
  64.6 54.5 all-gather.13
  120.8 45.9 all-gather.11
  172.0 74.5 all-gather.7

commit v4 on v3

--- a/solution.py
+++ b/solution.py
@@ -119,22 +119,30 @@
     grad_weights = jnp.sum(pick_table * per_slot[None, None, :], axis=-1)
     grad_logits = gate_back(grad_weights)[0]
     grad_router = jnp.dot(hidden.astype(jnp.float32).T, grad_logits, precision=HIGHEST)
-    router_parts = lax.all_to_all(
-        grad_router.astype(jnp.bfloat16).reshape(groups_dp, shard_rows, -1),
-        "dp",
-        split_axis=0,
-        concat_axis=0,
-        tiled=True,
-    )
-    router_part = jnp.sum(router_parts.astype(jnp.float32), axis=0)
-    router_mine = jnp.sum(small_gather(router_part, "expert"), axis=0)
     grad_hidden = jnp.dot(spread_half, grad_back, preferred_element_type=jnp.float32)
     grad_hidden = grad_hidden + jnp.dot(
         grad_logits, router_full.astype(jnp.float32).T, precision=HIGHEST
     )
     unused_value, norm_back = jax.vjp(normalize, inputs, norm_gain)
     grad_inputs, grad_gain = norm_back(grad_hidden)
-    gain_sum = jnp.sum(small_gather(grad_gain, ("dp", "expert")), axis=0)
+    scored = grad_router.shape[1]
+    gain_rows = D // scored
+    gain_high = lax.reduce_precision(grad_gain, 8, 7)
+    gain_pair = jnp.concatenate([gain_high, grad_gain - gain_high]).reshape(-1, scored)
+    sums = jnp.concatenate(
+        [
+            grad_router.reshape(groups_dp, shard_rows, scored),
+            jnp.broadcast_to(gain_pair[None], (groups_dp,) + gain_pair.shape),
+        ],
+        axis=1,
+    ).astype(jnp.bfloat16)
+    sums = lax.all_to_all(sums, "dp", split_axis=0, concat_axis=0, tiled=True)
+    part = jnp.sum(sums.astype(jnp.float32), axis=0)
+    gain_part = part[shard_rows : shard_rows + gain_rows] + part[shard_rows + gain_rows :]
+    part = jnp.concatenate([part[:shard_rows], gain_part], axis=0)
+    total = jnp.sum(small_gather(part, "expert"), axis=0)
+    router_mine = total[:shard_rows]
+    gain_sum = total[shard_rows:].reshape(-1)
     grad_rows_pair = lax.dot_general(
         rows_cut,
         units[:, : 2 * FF],

time: 272 us -> 264 us (0.971)
  starting transfers between devices: 21.6 us -> 17.1 us
    all_to_all x3 -> x2, waiting for transfers between devices: 28.3 us -> 17.4 us  [small_gather(): return lax.all_to_all(copies, axis, split_axis=0, concat_axis=0, tiled=True)]
    all_to_all x1, waiting for transfers between devices: 13.5 us -> 21.5 us  [body(): sums = lax.all_to_all(sums, 'dp', split_axis=0, concat_axis=0, tiled=True)]
    all_to_all x3 -> x2, starting transfers between devices: 13.8 us -> 9.79 us  [small_gather(): return lax.all_to_all(copies, axis, split_axis=0, concat_axis=0, tiled=True)]
    all_gather x1, waiting for transfers between devices: 29.8 us -> 32.8 us  [body(): w_down = lax.all_gather(down_weight[0], 'dp', axis=0, tiled=True)]
  transfers between devices with their start and end apart: 9 -> 8, of which waited for: 7 -> 6; matrix products, arithmetic and copies ran while one was open for 15% -> 15% of each run, Pallas kernels for 0% -> 0%
where the time goes in v4:
time: 264 us; the launch traced here: 263 us
  waiting for transfers between devices  131 us (50%)
  blocking collectives  49.6 us (19%)
  matrix products  33.5 us (13%)
  starting transfers between devices  17.1 us (6%)
  between operations  14.2 us (5%)
  other arithmetic  9.81 us (4%)
  local copies, waits for them, and re-layouts  7.97 us (3%)
    all_gather x1, waiting for transfers between devices, body(): w_up = lax.all_gather(up_weight[0], 'dp', axis=0, tiled=True)  43.8 us
    all_to_all x1, blocking collectives, body(): lax.all_to_all(cut.transpose(2, 0, 1, 3), 'dp', split_axis=0, concat_axis...  34.2 us
    all_gather x1, waiting for transfers between devices, body(): w_down = lax.all_gather(down_weight[0], 'dp', axis=0, tiled=True)  32.8 us
    all_to_all x1, waiting for transfers between devices, body(): sums = lax.all_to_all(sums, 'dp', split_axis=0, concat_axis=0, tiled=True)  21.5 us
    all_to_all x2, waiting for transfers between devices, small_gather(): return lax.all_to_all(copies, axis, split_axis=0, concat_axis=0, tiled=True)  17.4 us
    all_to_all x1, blocking collectives, body(): lax.all_to_all(leaving, 'expert', split_axis=0, concat_axis=0, tiled=True)  15.5 us
    all_to_all x1, waiting for transfers between devices, body(): lax.all_to_all(produced, 'expert', split_axis=0, concat_axis=0, tiled=True)  13.6 us
    all_to_all x2, starting transfers between devices, small_gather(): return lax.all_to_all(copies, axis, split_axis=0, concat_axis=0, tiled=True)  9.79 us
  transfers between devices with their start and end apart: 8, of which 6 were waited for; matrix products, arithmetic and copies ran while one was open for 15% of the time, Pallas kernels for 0%

profile of v4, /device:TPU:0, one launch (start us, length us, event | category | flops | bytes accessed | tf_op | source)
XLA Modules:
  0.0 263.4 jit_solution(10894384132849423158)
XLA Ops:
  9.4 1.5 broadcast_in_dim.25
  10.9 6.3 %all-to-all-start = ((bf16[8,256,64]{1,2,0:T(8,128)(2,1)}), bf16[8,256,64]{1,2,0:T(8,128)(2,1)S(1)}, u32[]{:S(2)}, u32[]{:S(2)}) async-start(bf16[8,256,64]{1,2,0:T(8,128)(2,1)} %broadcast_in_dim.25), calls=%async_computation | async-start | bytes 524288 | tf_op jit(solution)/shard_map/all_to_all | solution.py:47
  19.8 11.5 %all-to-all-done = bf16[8,256,64]{1,2,0:T(8,128)(2,1)S(1)} async-done(((bf16[8,256,64]{1,2,0:T(8,128)(2,1)}), bf16[8,256,64]{1,2,0:T(8,128)(2,1)S(1)}, u32[]{:S(2)}, u32[]{:S(2)}) %all-to-all-start) | async-done | bytes 262176 | tf_op jit(solution)/shard_map/all_to_all | solution.py:47
  33.5 15.5 %all_to_all.30 = bf16[4,2,32,2048]{3,2,1,0:T(8,128)(2,1)S(1)} all-to-all(bf16[4,2,32,2048]{3,2,1,0:T(8,128)(2,1)S(1)} %pad_maximum_fusion), channel_id=1, replica_groups=mesh['dp'=8,'expert'=4] {'expert'}, dimensions={0} | all-to-all | bytes 2097152 | tf_op jit(solution)/shard_map/all_to_all | solution.py:90
  49.7 34.2 %all_to_all.31 = bf16[8,2,128,256]{3,2,1,0:T(8,128)(2,1)} all-to-all(bf16[8,2,128,256]{3,2,1,0:T(8,128)(2,1)S(1)} %copy.105), channel_id=1, replica_groups=mesh['dp'=8,'expert'=4] {'dp'}, dimensions={0} | all-to-all | bytes 2097152 | tf_op jit(solution)/shard_map/all_to_all | solution.py:94
  83.8 2.9 %fusion.12 = f32[128,1024]{1,0:T(8,128)S(1)} fusion(bf16[128,2048]{1,0:T(8,128)(2,1)S(1)} %bitcast.89, bf16[1,2048,1024]{2,1,0:T(8,128)(2,1)} %all-gather.10.cloned.1.call-done), kind=kOutput, calls=%fused_computation.12 | convolution fusion | flops 536870912 | bytes 5242880 | tf_op jit(solution)/shard_map/dot_general | solution.py:51
  86.8 32.8 %all-gather.14.cloned.1.call-done = bf16[1,2048,1024]{2,1,0:T(8,128)(2,1)} async-done(((bf16[1,256,1024]{2,1,0:T(8,128)(2,1)}), bf16[1,2048,1024]{2,1,0:T(8,128)(2,1)}) %all-gather.14.cloned.1.call-update) | async-done | bytes 4194320 | tf_op jit(solution)/shard_map/all_gather | solution.py:72
  119.5 3.7 %fusion.2 = f32[128,1024]{1,0:T(8,128)} fusion(bf16[128,2048]{1,0:T(8,128)(2,1)S(1)} %bitcast.92, bf16[1,2048,1024]{2,1,0:T(8,128)(2,1)} %all-gather.14.cloned.1.call-done), kind=kOutput, calls=%fused_computation.2 | convolution fusion | flops 536870912 | bytes 5242880 | tf_op jit(solution)/shard_map/dot_general | solution.py:55
  123.2 43.8 %all-gather.12.cloned.1.call-done = bf16[1,2048,1024]{2,1,0:T(8,128)(2,1)} async-done(((bf16[1,256,1024]{2,1,0:T(8,128)(2,1)}), bf16[1,2048,1024]{2,1,0:T(8,128)(2,1)}) %all-gather.12.cloned.1.call-update) | async-done | bytes 4194320 | tf_op jit(solution)/shard_map/all_gather | solution.py:71
  167.0 3.2 %multiply_convert_fusion.2 = (bf16[128,1024]{1,0:T(8,128)(2,1)S(1)}, bf16[128,1024]{1,0:T(8,128)(2,1)S(1)}, bf16[128,1024]{1,0:T(8,128)(2,1)S(1)}) fusion(f32[128,1024]{1,0:T(8,128)S(1)} %fusion.12, f32[128,1024]{1,0:T(8,128)} %fusion.2, bf16[128,2048]{1,0:T(8,128)(2,1)S(1)} %bitcast.90, bf16[1,2048,1024]{2,1,0:T(8,128)(2,1)} %all-gather.12.cloned.1.call-done), kind=kOutput, calls=%fused_computation.56 | convolution fusion | flops 538968064 | bytes 6553600 | tf_op jit(solution)/shard_map/dot_general | solution.py:52
  171.3 3.8 %fusion.24 = bf16[128,2048]{1,0:T(8,128)(2,1)S(1)} fusion(bf16[128,1024]{1,0:T(8,128)(2,1)S(1)} %get-tuple-element.21, bf16[1,2048,1024]{2,1,0:T(8,128)(2,1)} %all-gather.14.cloned.1.call-done), kind=kOutput, calls=%fused_computation.21 | convolution fusion | flops 537133056 | bytes 4980736 | tf_op jit(solution)/shard_map/dot_general | solution.py:104
  175.1 3.9 %fusion.6 = f32[128,2048]{1,0:T(8,128)S(1)} fusion(bf16[128,1024]{1,0:T(8,128)(2,1)S(1)} %get-tuple-element.23, bf16[1,2048,1024]{2,1,0:T(8,128)(2,1)} %all-gather.12.cloned.1.call-done), kind=kOutput, calls=%fused_computation.6 | convolution fusion | flops 536870912 | bytes 5505024 | tf_op jit(solution)/shard_map/dot_general | solution.py:107
  179.0 1.5 fusion.21
  181.7 3.7 %all-to-all-start.3 = ((bf16[4,2,32,2048]{3,2,1,0:T(8,128)(2,1)}), bf16[4,2,32,2048]{3,2,1,0:T(8,128)(2,1)S(1)}, u32[]{:S(2)}, u32[]{:S(2)}) async-start(bf16[4,2,32,2048]{3,2,1,0:T(8,128)(2,1)} %pad_maximum_fusion.1), calls=%async_computation.3 | async-start | bytes 2097152 | tf_op jit(solution)/shard_map/all_to_all | solution.py:112
  185.9 13.6 %all-to-all-done.3 = bf16[4,2,32,2048]{3,2,1,0:T(8,128)(2,1)S(1)} async-done(((bf16[4,2,32,2048]{3,2,1,0:T(8,128)(2,1)}), bf16[4,2,32,2048]{3,2,1,0:T(8,128)(2,1)S(1)}, u32[]{:S(2)}, u32[]{:S(2)}) %all-to-all-start.3) | async-done | bytes 1048608 | tf_op jit(solution)/shard_map/all_to_all | solution.py:112
  203.6 1.6 fusion.42
  206.1 2.3 fusion.53
  210.1 3.5 %all-to-all-start.4 = ((bf16[8,320,64]{1,2,0:T(8,128)(2,1)}), bf16[8,320,64]{1,2,0:T(8,128)(2,1)S(1)}, u32[]{:S(2)}, u32[]{:S(2)}) async-start(bf16[8,320,64]{1,2,0:T(8,128)(2,1)} %pad_maximum_fusion.3), calls=%async_computation.4 | async-start | bytes 786432 | tf_op jit(solution)/shard_map/all_to_all | solution.py:139
  214.5 21.5 %all-to-all-done.4 = bf16[8,320,64]{1,2,0:T(8,128)(2,1)S(1)} async-done(((bf16[8,320,64]{1,2,0:T(8,128)(2,1)}), bf16[8,320,64]{1,2,0:T(8,128)(2,1)S(1)}, u32[]{:S(2)}, u32[]{:S(2)}) %all-to-all-start.4) | async-done | bytes 327712 | tf_op jit(solution)/shard_map/all_to_all | solution.py:139
  236.9 3.5 %all-to-all-start.5 = ((f32[4,288,64]{1,2,0:T(8,128)}), f32[4,288,64]{1,2,0:T(8,128)S(1)}, u32[]{:S(2)}, u32[]{:S(2)}) async-start(f32[4,288,64]{1,2,0:T(8,128)} %broadcast_in_dim.31), calls=%async_computation.5 | async-start | bytes 786432 | tf_op jit(solution)/shard_map/all_to_all | solution.py:47
  240.4 1.4 convolution_convert_fusion
  241.7 5.9 %all-to-all-done.5 = f32[4,288,64]{1,2,0:T(8,128)S(1)} async-done(((f32[4,288,64]{1,2,0:T(8,128)}), f32[4,288,64]{1,2,0:T(8,128)S(1)}, u32[]{:S(2)}, u32[]{:S(2)}) %all-to-all-start.5) | async-done | bytes 294944 | tf_op jit(solution)/shard_map/all_to_all | solution.py:47
  249.1 3.6 %fusion.15 = bf16[256,2048]{1,0:T(8,128)(2,1)S(1)} fusion(bf16[1024,256]{1,0:T(8,128)(2,1)} %bitcast.107, bf16[1024,3072]{1,0:T(8,128)(2,1)} %all-gather.8.cloned.1.call-done), kind=kOutput, calls=%fused_computation.16 | convolution fusion | flops 1074266112 | bytes 5767168 | tf_op jit(solution)/shard_map/dot_general | solution.py:146
  253.7 3.1 %fusion.35 = bf16[1,256,1024]{2,1,0:T(8,128)(2,1)} fusion(bf16[1024,256]{1,0:T(8,128)(2,1)S(1)} %bitcast.102, bf16[1024,3072]{1,0:T(8,128)(2,1)} %all-gather.8.cloned.1.call-done), kind=kOutput, calls=%fused_computation.36 | convolution fusion | flops 537133056 | bytes 3145728 | tf_op jit(solution)/shard_map/dot_general | solution.py:152
  (87 shorter events, 21.0 us)
Async XLA Ops:
  7.2 25.6 %copy-start = (bf16[128,2048]{1,0:T(8,128)(2,1)S(1)}, bf16[128,2048]{1,0:T(8,128)(2,1)}, u32[]{:S(2)}) copy-start(bf16[128,2048]{1,0:T(8,128)(2,1)} %param.15) | copy-start | bytes 1572868
  7.2 24.6 %copy-start.6 = (s32[128,8]{0,1:T(8,128)S(1)}, s32[128,8]{0,1:T(8,128)}, u32[]{:S(2)}) copy-start(s32[128,8]{0,1:T(8,128)} %param.11) | copy-start | bytes 12292
  7.2 12.4 %copy-start.2 = (bf16[128,2048]{1,0:T(8,128)(2,1)S(1)}, bf16[128,2048]{1,0:T(8,128)(2,1)}, u32[]{:S(2)}) copy-start(bf16[128,2048]{1,0:T(8,128)(2,1)} %param.8) | copy-start | bytes 1572868
  7.2 24.2 %copy-start.5 = (f32[2048]{0:T(1024)S(1)}, f32[2048]{0:T(1024)}, u32[]{:S(2)}) copy-start(f32[2048]{0:T(1024)} %param.9) | copy-start | bytes 24580
  7.2 76.6 %all-gather.10.cloned.1.call-start = ((), (), s32[]{:S(2)}) async-start(), calls=%async_computation.7 | async-start | bytes 4718592 | tf_op jit(solution)/shard_map/all_gather | solution.py:70
  7.9 111.6 %all-gather.14.cloned.1.call-start = ((), (), s32[]{:S(2)}) async-start(), calls=%async_computation.9 | async-start | bytes 4718592 | tf_op jit(solution)/shard_map/all_gather | solution.py:72
  8.7 158.3 %all-gather.12.cloned.1.call-start = ((), (), s32[]{:S(2)}) async-start(), calls=%async_computation.8 | async-start | bytes 4718592 | tf_op jit(solution)/shard_map/all_gather | solution.py:71
  10.9 20.4 %all-to-all-start = ((bf16[8,256,64]{1,2,0:T(8,128)(2,1)}), bf16[8,256,64]{1,2,0:T(8,128)(2,1)S(1)}, u32[]{:S(2)}, u32[]{:S(2)}) async-start(bf16[8,256,64]{1,2,0:T(8,128)(2,1)} %broadcast_in_dim.25), calls=%async_computation | async-start | bytes 524288 | tf_op jit(solution)/shard_map/all_to_all | solution.py:47
  17.2 231.8 %all-gather.8.cloned.1.call-start = ((), (), s32[]{:S(2)}) async-start(), calls=%async_computation.6 | async-start | bytes 7077888 | tf_op jit(solution)/shard_map/all_gather | solution.py:101
  19.8 11.6 %copy-start.9 = (f32[128]{0:T(128)}, f32[128]{0:T(128)S(1)}, u32[]{:S(2)}) copy-start(f32[128]{0:T(128)S(1)} %fusion.44) | copy-start | bytes 1540
  19.8 29.2 %copy-start.8 = (f32[128]{0:T(128)}, f32[128]{0:T(128)S(1)}, u32[]{:S(2)}) copy-start(f32[128]{0:T(128)S(1)} %fusion.48) | copy-start | bytes 1540
  31.8 153.5 %copy-start.7 = (f32[128]{0:T(128)}, f32[128]{0:T(128)S(1)}, u32[]{:S(2)}) copy-start(f32[128]{0:T(128)S(1)} %exponential_reduce_fusion) | copy-start | bytes 1540
  32.3 1.1 copy-start.4
  171.2 7.8 %copy-start.1 = (bf16[1,2048,1024]{2,1,0:T(8,128)(2,1)S(1)}, bf16[1,2048,1024]{2,1,0:T(8,128)(2,1)}, u32[]{:S(2)}) copy-start(bf16[1,2048,1024]{2,1,0:T(8,128)(2,1)} %all-gather.10.cloned.1.call-done) | copy-start | bytes 12582916
  181.7 17.8 %all-to-all-start.3 = ((bf16[4,2,32,2048]{3,2,1,0:T(8,128)(2,1)}), bf16[4,2,32,2048]{3,2,1,0:T(8,128)(2,1)S(1)}, u32[]{:S(2)}, u32[]{:S(2)}) async-start(bf16[4,2,32,2048]{3,2,1,0:T(8,128)(2,1)} %pad_maximum_fusion.1), calls=%async_computation.3 | async-start | bytes 2097152 | tf_op jit(solution)/shard_map/all_to_all | solution.py:112
  208.4 5.2 %copy-start.3 = (bf16[8,2,128,256]{3,2,1,0:T(8,128)(2,1)S(1)}, bf16[8,2,128,256]{3,2,1,0:T(8,128)(2,1)}, u32[]{:S(2)}) copy-start(bf16[8,2,128,256]{3,2,1,0:T(8,128)(2,1)} %all_to_all.31) | copy-start | bytes 3145732
  210.1 25.9 %all-to-all-start.4 = ((bf16[8,320,64]{1,2,0:T(8,128)(2,1)}), bf16[8,320,64]{1,2,0:T(8,128)(2,1)S(1)}, u32[]{:S(2)}, u32[]{:S(2)}) async-start(bf16[8,320,64]{1,2,0:T(8,128)(2,1)} %pad_maximum_fusion.3), calls=%async_computation.4 | async-start | bytes 786432 | tf_op jit(solution)/shard_map/all_to_all | solution.py:139
  236.9 10.7 %all-to-all-start.5 = ((f32[4,288,64]{1,2,0:T(8,128)}), f32[4,288,64]{1,2,0:T(8,128)S(1)}, u32[]{:S(2)}, u32[]{:S(2)}) async-start(f32[4,288,64]{1,2,0:T(8,128)} %broadcast_in_dim.31), calls=%async_computation.5 | async-start | bytes 786432 | tf_op jit(solution)/shard_map/all_to_all | solution.py:47
Sparse Core Ops, SparseCore 0:
  9.6 54.2 all-gather.9
  65.5 53.9 all-gather.13
  121.1 45.8 all-gather.11
  171.4 71.7 all-gather.7
